TPU v7x, 256 devices: a whole 4x4x8 slice. The times are simulated.
256 devices in a mesh: segment: 4 (over y_hi, core), frame: 64 (over x, z, y_lo).
Axes of the slice: x: 4, y: 4 (y_hi: 2, y_lo: 2; y = y_hi * 2 + y_lo), z: 8, core: 2. Of those that a mesh axis runs over, the one named last changes fastest.
Arguments:
- clips: bfloat16 [4, 64, 320, 1024], P('segment', 'frame'), may hold values from -6 to 6
- timesteps: int32 [4], replicated, may hold values from 0 to 999
- gain: float32 [4, 320], replicated, may hold values from 0.25 to 1.75
- temporal_weight: bfloat16 [4, 3, 320, 320], P('segment'), may hold values from -0.1875 to 0.1875
- film_weight: bfloat16 [4, 320, 320], P('segment'), may hold values from -0.3125 to 0.3125
- out_weight: bfloat16 [4, 320, 320], P('segment'), may hold values from -0.3125 to 0.3125
- skip_weight: bfloat16 [2, 320, 320], replicated, may hold values from -0.3125 to 0.3125
Outputs:
- video_out: bfloat16 [4, 64, 320, 1024], P('segment', 'frame')
All inputs are finite; a program needn't handle non-finite values.
Results may differ from a plain program's by a relative error of at most 0.012.
Values may be sent and summed in bfloat16 or wider, within the bound.
A program may use at most 64 MiB of HBM per device.

v0:
```python
import math

import jax
import jax.numpy as jnp
from jax import lax
from jax.sharding import PartitionSpec as P


def extended(cells, sides, width):
    for axis, dim in sides:
        count = lax.axis_size(axis)
        ends = count - 1
        head = lax.slice_in_dim(cells, 0, width, axis=dim)
        tail = lax.slice_in_dim(cells, cells.shape[dim] - width, cells.shape[dim], axis=dim)
        cells = jnp.concatenate(
            [
                lax.ppermute(tail, axis, [(i, (i + 1) % count) for i in range(ends)]),
                cells,
                lax.ppermute(head, axis, [((i + 1) % count, i) for i in range(ends)]),
            ],
            axis=dim,
        )
    return cells


def shifted(array, axis, by):
    length = lax.axis_size(axis)
    pairs = [(i, i + by) for i in range(length) if 0 <= i + by < length]
    return lax.ppermute(array, axis, pairs)


def embed(timesteps, width):
    half = width // 2
    freq = jnp.exp(-math.log(10000.0) * jnp.arange(half, dtype=jnp.float32) / half)
    angle = timesteps.astype(jnp.float32)[:, None] * freq[None, :]
    return jnp.concatenate([jnp.sin(angle), jnp.cos(angle)], axis=-1).astype(jnp.bfloat16)


def channel_mix(weight, field):
    return jnp.einsum("io,fip->fop", weight, field, preferred_element_type=jnp.float32)


def temporal_mix(normed, taps):
    padded = extended(normed, (("frame", 0),), 1)
    count = normed.shape[0]
    mixed = channel_mix(taps[0], padded[0:count])
    mixed = mixed + channel_mix(taps[1], padded[1 : count + 1])
    mixed = mixed + channel_mix(taps[2], padded[2 : count + 2])
    return mixed


def section_core(state, own_gain, taps, film_vec, projection):
    values = state.astype(jnp.float32)
    meansq = jnp.mean(values * values, axis=1, keepdims=True)
    normed = (values * lax.rsqrt(meansq + 1e-05) * own_gain[None, :, None]).astype(jnp.bfloat16)
    mixed = temporal_mix(normed, taps)
    hidden = jax.nn.silu(mixed * (1.0 + film_vec[None, :, None])).astype(jnp.bfloat16)
    return values + channel_mix(projection, hidden)


def shards(clips, timesteps, gain, temporal_weight, film_weight, out_weight, skip_weight):
    sections = lax.axis_size("segment")
    section = lax.axis_index("segment")
    emb = embed(timesteps, clips.shape[2])
    all_clips = lax.all_gather(clips, "segment", axis=0, tiled=True)
    batches = all_clips.shape[0]
    film_all = jnp.dot(emb, film_weight[0], preferred_element_type=jnp.float32)
    own_gain = lax.dynamic_index_in_dim(gain, section, 0, keepdims=False)
    taps = temporal_weight[0]
    projection = out_weight[0]
    decoder_weight = jnp.where(section == sections - 1, skip_weight[1], skip_weight[0])
    is_first = section == 0
    is_decoder = section >= 2
    empty = jnp.zeros(all_clips.shape[1:], jnp.bfloat16)
    handed = empty
    carried = empty
    finals = []
    steps_total = batches + sections - 1
    for step in range(steps_total):
        source = all_clips[step] if step < batches else empty
        state = jnp.where(is_first, source, handed)
        micro = step - section
        select = jnp.arange(batches) == micro
        film_vec = jnp.sum(jnp.where(select[:, None], film_all, 0.0), axis=0)
        far_skip = empty
        if step >= 3 and step - 3 < batches:
            far_skip = all_clips[step - 3]
        skip_in = jnp.where(section == sections - 1, far_skip, carried)
        total = section_core(state, own_gain, taps, film_vec, projection)
        skip_term = channel_mix(decoder_weight, skip_in)
        total = total + jnp.where(is_decoder, skip_term, 0.0)
        result = total.astype(jnp.bfloat16)
        if step >= sections - 1:
            finals.append(result)
        if step < steps_total - 1:
            handed, carried = shifted((result, state), "segment", 1)
    stacked = jnp.stack(finals, axis=0).astype(jnp.float32)
    stacked = jnp.where(section == sections - 1, stacked, 0.0)
    return lax.psum_scatter(
        stacked.astype(jnp.bfloat16), "segment", scatter_dimension=0, tiled=True
    )


def solution(mesh):
    placed = (
        P("segment", "frame", None, None),
        P(),
        P(),
        P("segment", None, None, None),
        P("segment", None, None),
        P("segment", None, None),
        P(),
    )
    return jax.shard_map(
        shards,
        mesh=mesh,
        in_specs=placed,
        out_specs=P("segment", "frame", None, None),
        check_vma=False,
    )
```

profile of v0, /device:TPU:18, one launch (start us, length us, event | category | flops | bytes accessed | tf_op | source)
XLA Modules:
  0.0 449.8 jit_solution(10235497476458363797)
XLA Ops:
  10.0 31.7 %all-gather.2.cloned.1.call-done = bf16[4,1,320,1024]{3,2,1,0:T(8,128)(2,1)} async-done(((bf16[1,1,320,1024]{3,2,1,0:T(8,128)(2,1)}), bf16[4,1,320,1024]{3,2,1,0:T(8,128)(2,1)}) %all-gather.2.cloned.1.call-update) | async-done | bytes 2621456 | tf_op jit(solution)/shard_map/all_gather | solution.py:65
  43.2 6.7 %collective-permute-start.1 = (bf16[1,320,1024]{2,1,0:T(8,128)(2,1)S(1)}, bf16[1,320,1024]{2,1,0:T(8,128)(2,1)S(1)}, u32[]{:S(2)}, u32[]{:S(2)}) collective-permute-start(bf16[1,320,1024]{2,1,0:T(8,128)(2,1)S(1)} %fusion.51), channel_id=1, source_target_pairs={{1,0},{2,1},{3,2},{4,3},{5,4},{6,5},{7,6},{8,7},{9,8},{10,9},{11,1... | collective-permute-start | bytes 1966088 | tf_op jit(solution)/shard_map/ppermute | solution.py:19
  50.2 1.9 collective-permute-start
  52.1 2.8 fusion.81
  54.9 21.4 %collective-permute-done.1 = bf16[1,320,1024]{2,1,0:T(8,128)(2,1)S(1)} collective-permute-done((bf16[1,320,1024]{2,1,0:T(8,128)(2,1)S(1)}, bf16[1,320,1024]{2,1,0:T(8,128)(2,1)S(1)}, u32[]{:S(2)}, u32[]{:S(2)}) %collective-permute-start.1) | collective-permute-done | bytes 655392 | tf_op jit(solution)/shard_map/ppermute | solution.py:19
  78.0 3.1 convert_add_fusion.6
  81.5 1.9 collective-permute-start.2
  83.5 1.9 collective-permute-start.5
  85.4 9.6 %collective-permute-done.2 = bf16[1,320,1024]{2,1,0:T(8,128)(2,1)S(1)} collective-permute-done((bf16[1,320,1024]{2,1,0:T(8,128)(2,1)S(1)}, bf16[1,320,1024]{2,1,0:T(8,128)(2,1)S(1)}, u32[]{:S(2)}, u32[]{:S(2)}) %collective-permute-start.2) | collective-permute-done | bytes 655392 | tf_op jit(solution)/shard_map/ppermute | solution.py:29
  96.5 8.6 %collective-permute-start.4 = (bf16[1,320,1024]{2,1,0:T(8,128)(2,1)S(1)}, bf16[1,320,1024]{2,1,0:T(8,128)(2,1)S(1)}, u32[]{:S(2)}, u32[]{:S(2)}) collective-permute-start(bf16[1,320,1024]{2,1,0:T(8,128)(2,1)S(1)} %fusion.54), channel_id=1, source_target_pairs={{1,0},{2,1},{3,2},{4,3},{5,4},{6,5},{7,6},{8,7},{9,8},{10,9},{11,1... | collective-permute-start | bytes 1966088 | tf_op jit(solution)/shard_map/ppermute | solution.py:19
  105.2 1.9 collective-permute-start.3
  107.1 15.3 %collective-permute-done.5 = bf16[1,320,1024]{2,1,0:T(8,128)(2,1)S(1)} collective-permute-done((bf16[1,320,1024]{2,1,0:T(8,128)(2,1)S(1)}, bf16[1,320,1024]{2,1,0:T(8,128)(2,1)S(1)}, u32[]{:S(2)}, u32[]{:S(2)}) %collective-permute-start.5) | collective-permute-done | bytes 655392 | tf_op jit(solution)/shard_map/ppermute | solution.py:29
  127.3 3.5 fusion.47
  130.8 1.9 collective-permute-start.6
  132.7 1.9 collective-permute-start.9
  134.6 10.6 %collective-permute-done.6 = bf16[1,320,1024]{2,1,0:T(8,128)(2,1)S(1)} collective-permute-done((bf16[1,320,1024]{2,1,0:T(8,128)(2,1)S(1)}, bf16[1,320,1024]{2,1,0:T(8,128)(2,1)S(1)}, u32[]{:S(2)}, u32[]{:S(2)}) %collective-permute-start.6) | collective-permute-done | bytes 655392 | tf_op jit(solution)/shard_map/ppermute | solution.py:29
  146.8 7.5 %collective-permute-start.8 = (bf16[1,320,1024]{2,1,0:T(8,128)(2,1)S(1)}, bf16[1,320,1024]{2,1,0:T(8,128)(2,1)S(1)}, u32[]{:S(2)}, u32[]{:S(2)}) collective-permute-start(bf16[1,320,1024]{2,1,0:T(8,128)(2,1)S(1)} %fusion.57), channel_id=1, source_target_pairs={{1,0},{2,1},{3,2},{4,3},{5,4},{6,5},{7,6},{8,7},{9,8},{10,9},{11,1... | collective-permute-start | bytes 1966088 | tf_op jit(solution)/shard_map/ppermute | solution.py:19
  154.3 1.9 collective-permute-start.7
  156.2 16.8 %collective-permute-done.9 = bf16[1,320,1024]{2,1,0:T(8,128)(2,1)S(1)} collective-permute-done((bf16[1,320,1024]{2,1,0:T(8,128)(2,1)S(1)}, bf16[1,320,1024]{2,1,0:T(8,128)(2,1)S(1)}, u32[]{:S(2)}, u32[]{:S(2)}) %collective-permute-start.9) | collective-permute-done | bytes 655392 | tf_op jit(solution)/shard_map/ppermute | solution.py:29
  176.9 3.9 fusion.46
  184.6 11.0 %collective-permute-done.10 = bf16[1,320,1024]{2,1,0:T(8,128)(2,1)S(1)} collective-permute-done((bf16[1,320,1024]{2,1,0:T(8,128)(2,1)}, bf16[1,320,1024]{2,1,0:T(8,128)(2,1)S(1)}, u32[]{:S(2)}, u32[]{:S(2)}) %collective-permute-start.10) | collective-permute-done | bytes 655392 | tf_op jit(solution)/shard_map/ppermute | solution.py:29
  197.3 7.9 %collective-permute-start.12 = (bf16[1,320,1024]{2,1,0:T(8,128)(2,1)S(1)}, bf16[1,320,1024]{2,1,0:T(8,128)(2,1)S(1)}, u32[]{:S(2)}, u32[]{:S(2)}) collective-permute-start(bf16[1,320,1024]{2,1,0:T(8,128)(2,1)S(1)} %fusion.60), channel_id=1, source_target_pairs={{1,0},{2,1},{3,2},{4,3},{5,4},{6,5},{7,6},{8,7},{9,8},{10,9},{11,1... | collective-permute-start | bytes 1966088 | tf_op jit(solution)/shard_map/ppermute | solution.py:19
  205.1 2.1 collective-permute-start.11
  207.2 16.0 %collective-permute-done.13 = bf16[1,320,1024]{2,1,0:T(8,128)(2,1)S(1)} collective-permute-done((bf16[1,320,1024]{2,1,0:T(8,128)(2,1)S(1)}, bf16[1,320,1024]{2,1,0:T(8,128)(2,1)S(1)}, u32[]{:S(2)}, u32[]{:S(2)}) %collective-permute-start.13) | collective-permute-done | bytes 655392 | tf_op jit(solution)/shard_map/ppermute | solution.py:29
  223.3 2.7 fusion.31
  229.3 3.5 fusion.45
  236.7 17.0 %collective-permute-done.14 = bf16[1,320,1024]{2,1,0:T(8,128)(2,1)S(1)} collective-permute-done((bf16[1,320,1024]{2,1,0:T(8,128)(2,1)S(1)}, bf16[1,320,1024]{2,1,0:T(8,128)(2,1)S(1)}, u32[]{:S(2)}, u32[]{:S(2)}) %collective-permute-start.14) | collective-permute-done | bytes 655392 | tf_op jit(solution)/shard_map/ppermute | solution.py:29
  256.1 3.9 collective-permute-start.15
  260.0 14.3 %collective-permute-done.17 = bf16[1,320,1024]{2,1,0:T(8,128)(2,1)S(1)} collective-permute-done((bf16[1,320,1024]{2,1,0:T(8,128)(2,1)S(1)}, bf16[1,320,1024]{2,1,0:T(8,128)(2,1)S(1)}, u32[]{:S(2)}, u32[]{:S(2)}) %collective-permute-start.17) | collective-permute-done | bytes 655392 | tf_op jit(solution)/shard_map/ppermute | solution.py:29
  274.3 2.7 fusion.30
  279.2 3.9 fusion.44
  285.1 1.9 collective-permute-start.21
  287.0 10.2 %collective-permute-done.18 = bf16[1,320,1024]{2,1,0:T(8,128)(2,1)S(1)} collective-permute-done((bf16[1,320,1024]{2,1,0:T(8,128)(2,1)}, bf16[1,320,1024]{2,1,0:T(8,128)(2,1)S(1)}, u32[]{:S(2)}, u32[]{:S(2)}) %collective-permute-start.18) | collective-permute-done | bytes 655392 | tf_op jit(solution)/shard_map/ppermute | solution.py:29
  297.6 7.5 %collective-permute-start.20 = (bf16[1,320,1024]{2,1,0:T(8,128)(2,1)S(1)}, bf16[1,320,1024]{2,1,0:T(8,128)(2,1)S(1)}, u32[]{:S(2)}, u32[]{:S(2)}) collective-permute-start(bf16[1,320,1024]{2,1,0:T(8,128)(2,1)S(1)} %fusion.66), channel_id=1, source_target_pairs={{1,0},{2,1},{3,2},{4,3},{5,4},{6,5},{7,6},{8,7},{9,8},{10,9},{11,1... | collective-permute-start | bytes 1966088 | tf_op jit(solution)/shard_map/ppermute | solution.py:19
  305.1 1.9 collective-permute-start.19
  307.1 9.5 %collective-permute-done.21 = bf16[1,320,1024]{2,1,0:T(8,128)(2,1)S(1)} collective-permute-done((bf16[1,320,1024]{2,1,0:T(8,128)(2,1)S(1)}, bf16[1,320,1024]{2,1,0:T(8,128)(2,1)S(1)}, u32[]{:S(2)}, u32[]{:S(2)}) %collective-permute-start.21) | collective-permute-done | bytes 655392 | tf_op jit(solution)/shard_map/ppermute | solution.py:29
  316.5 2.7 fusion.29
  320.9 2.9 collective-permute-done.20
  325.4 3.5 fusion.43
  332.8 14.3 %collective-permute-done.22 = bf16[1,320,1024]{2,1,0:T(8,128)(2,1)S(1)} collective-permute-done((bf16[1,320,1024]{2,1,0:T(8,128)(2,1)S(1)}, bf16[1,320,1024]{2,1,0:T(8,128)(2,1)S(1)}, u32[]{:S(2)}, u32[]{:S(2)}) %collective-permute-start.22) | collective-permute-done | bytes 655392 | tf_op jit(solution)/shard_map/ppermute | solution.py:29
  347.5 9.5 %collective-permute-start.24 = (bf16[1,320,1024]{2,1,0:T(8,128)(2,1)S(1)}, bf16[1,320,1024]{2,1,0:T(8,128)(2,1)S(1)}, u32[]{:S(2)}, u32[]{:S(2)}) collective-permute-start(bf16[1,320,1024]{2,1,0:T(8,128)(2,1)S(1)} %fusion.69), channel_id=1, source_target_pairs={{1,0},{2,1},{3,2},{4,3},{5,4},{6,5},{7,6},{8,7},{9,8},{10,9},{11,1... | collective-permute-start | bytes 1966088 | tf_op jit(solution)/shard_map/ppermute | solution.py:19
  356.9 2.1 collective-permute-start.23
  359.1 3.1 collective-permute-done.25
  362.2 2.7 fusion.28
  365.5 9.3 %collective-permute-done.24 = bf16[1,320,1024]{2,1,0:T(8,128)(2,1)S(1)} collective-permute-done((bf16[1,320,1024]{2,1,0:T(8,128)(2,1)S(1)}, bf16[1,320,1024]{2,1,0:T(8,128)(2,1)S(1)}, u32[]{:S(2)}, u32[]{:S(2)}) %collective-permute-start.24) | collective-permute-done | bytes 655392 | tf_op jit(solution)/shard_map/ppermute | solution.py:19
  376.6 3.9 fusion.72
  380.5 3.1 select_convert_fusion
  383.6 59.3 %reduce-scatter.2.cloned.1.call-done = bf16[1,1,320,1024]{3,2,1,0:T(8,128)(2,1)} async-done(((bf16[4,1,320,1024]{3,2,1,0:T(8,128)(2,1)}), bf16[1,1,320,1024]{3,2,1,0:T(8,128)(2,1)}) %reduce-scatter.2.cloned.1.call-update) | async-done | bytes 655376 | tf_op jit(solution)/shard_map/reduce_scatter | solution.py:99
  (87 shorter events, 48.5 us)
Async XLA Ops:
  6.5 71.4 %copy-start = (bf16[1,320,320]{2,1,0:T(8,128)(2,1)S(1)}, bf16[1,320,320]{2,1,0:T(8,128)(2,1)}, u32[]{:S(2)}) copy-start(bf16[1,320,320]{2,1,0:T(8,128)(2,1)} %param.12) | copy-start | bytes 614404
  6.5 35.1 %all-gather.2.cloned.1.call-start = ((), (), s32[]{:S(2)}) async-start(), calls=%async_computation.1 | async-start | bytes 3276800 | tf_op jit(solution)/shard_map/all_gather | solution.py:65
  7.3 435.7 %reduce-scatter.2.cloned.1.call-start = ((), (), s32[]{:S(2)}) async-start(), calls=%async_computation.2 | async-start | bytes 3276800 | tf_op jit(solution)/shard_map/reduce_scatter | solution.py:99
  10.0 40.0 %copy-start.4 = (bf16[1,320,320]{2,1,0:T(8,128)(2,1)S(1)}, bf16[1,320,320]{2,1,0:T(8,128)(2,1)}, u32[]{:S(2)}) copy-start(bf16[1,320,320]{2,1,0:T(8,128)(2,1)} %param.11) | copy-start | bytes 614404
  10.0 42.1 %copy-start.1 = (bf16[1,3,320,320]{3,2,1,0:T(8,128)(2,1)S(1)}, bf16[1,3,320,320]{3,2,1,0:T(8,128)(2,1)}, u32[]{:S(2)}) copy-start(bf16[1,3,320,320]{3,2,1,0:T(8,128)(2,1)} %param.10) | copy-start | bytes 1843204
  43.2 33.2 %collective-permute-start.1 = (bf16[1,320,1024]{2,1,0:T(8,128)(2,1)S(1)}, bf16[1,320,1024]{2,1,0:T(8,128)(2,1)S(1)}, u32[]{:S(2)}, u32[]{:S(2)}) collective-permute-start(bf16[1,320,1024]{2,1,0:T(8,128)(2,1)S(1)} %fusion.51), channel_id=1, source_target_pairs={{1,0},{2,1},{3,2},{4,3},{5,4},{6,5},{7,6},{8,7},{9,8},{10,9},{11,1... | collective-permute-start | bytes 1966088 | tf_op jit(solution)/shard_map/ppermute | solution.py:19
  50.2 27.8 %collective-permute-start = (bf16[1,320,1024]{2,1,0:T(8,128)(2,1)S(1)}, bf16[1,320,1024]{2,1,0:T(8,128)(2,1)}, u32[]{:S(2)}, u32[]{:S(2)}) collective-permute-start(bf16[1,320,1024]{2,1,0:T(8,128)(2,1)S(1)} %fusion.51), channel_id=1, source_target_pairs={{0,1},{1,2},{2,3},{3,4},{4,5},{5,6},{6,7},{7,8},{8,9},{9,10},{10,1... | collective-permute-start | bytes 1966088 | tf_op jit(solution)/shard_map/ppermute | solution.py:17
  81.5 13.4 %collective-permute-start.2 = (bf16[1,320,1024]{2,1,0:T(8,128)(2,1)S(1)}, bf16[1,320,1024]{2,1,0:T(8,128)(2,1)S(1)}, u32[]{:S(2)}, u32[]{:S(2)}) collective-permute-start(bf16[1,320,1024]{2,1,0:T(8,128)(2,1)S(1)} %fusion.48), channel_id=1, source_target_pairs={{0,64},{64,128},{128,192},{1,65},{65,129},{129,193},{2,66},{66,130... | collective-permute-start | bytes 1966088 | tf_op jit(solution)/shard_map/ppermute | solution.py:29
  83.5 38.9 %collective-permute-start.5 = (bf16[1,320,1024]{2,1,0:T(8,128)(2,1)S(1)}, bf16[1,320,1024]{2,1,0:T(8,128)(2,1)S(1)}, u32[]{:S(2)}, u32[]{:S(2)}) collective-permute-start(bf16[1,320,1024]{2,1,0:T(8,128)(2,1)S(1)} %get-tuple-element.23), channel_id=1, source_target_pairs={{0,64},{64,128},{128,192},{1,65},{65,129},{129,193},{2,66},{66,130... | collective-permute-start | bytes 1966088 | tf_op jit(solution)/shard_map/ppermute | solution.py:29
  96.5 29.1 %collective-permute-start.4 = (bf16[1,320,1024]{2,1,0:T(8,128)(2,1)S(1)}, bf16[1,320,1024]{2,1,0:T(8,128)(2,1)S(1)}, u32[]{:S(2)}, u32[]{:S(2)}) collective-permute-start(bf16[1,320,1024]{2,1,0:T(8,128)(2,1)S(1)} %fusion.54), channel_id=1, source_target_pairs={{1,0},{2,1},{3,2},{4,3},{5,4},{6,5},{7,6},{8,7},{9,8},{10,9},{11,1... | collective-permute-start | bytes 1966088 | tf_op jit(solution)/shard_map/ppermute | solution.py:19
  105.2 22.1 %collective-permute-start.3 = (bf16[1,320,1024]{2,1,0:T(8,128)(2,1)S(1)}, bf16[1,320,1024]{2,1,0:T(8,128)(2,1)}, u32[]{:S(2)}, u32[]{:S(2)}) collective-permute-start(bf16[1,320,1024]{2,1,0:T(8,128)(2,1)S(1)} %fusion.54), channel_id=1, source_target_pairs={{0,1},{1,2},{2,3},{3,4},{4,5},{5,6},{6,7},{7,8},{8,9},{9,10},{10,1... | collective-permute-start | bytes 1966088 | tf_op jit(solution)/shard_map/ppermute | solution.py:17
  130.8 14.5 %collective-permute-start.6 = (bf16[1,320,1024]{2,1,0:T(8,128)(2,1)S(1)}, bf16[1,320,1024]{2,1,0:T(8,128)(2,1)S(1)}, u32[]{:S(2)}, u32[]{:S(2)}) collective-permute-start(bf16[1,320,1024]{2,1,0:T(8,128)(2,1)S(1)} %fusion.47), channel_id=1, source_target_pairs={{0,64},{64,128},{128,192},{1,65},{65,129},{129,193},{2,66},{66,130... | collective-permute-start | bytes 1966088 | tf_op jit(solution)/shard_map/ppermute | solution.py:29
  132.7 40.4 %collective-permute-start.9 = (bf16[1,320,1024]{2,1,0:T(8,128)(2,1)S(1)}, bf16[1,320,1024]{2,1,0:T(8,128)(2,1)S(1)}, u32[]{:S(2)}, u32[]{:S(2)}) collective-permute-start(bf16[1,320,1024]{2,1,0:T(8,128)(2,1)S(1)} %get-tuple-element.21), channel_id=1, source_target_pairs={{0,64},{64,128},{128,192},{1,65},{65,129},{129,193},{2,66},{66,130... | collective-permute-start | bytes 1966088 | tf_op jit(solution)/shard_map/ppermute | solution.py:29
  146.8 28.4 %collective-permute-start.8 = (bf16[1,320,1024]{2,1,0:T(8,128)(2,1)S(1)}, bf16[1,320,1024]{2,1,0:T(8,128)(2,1)S(1)}, u32[]{:S(2)}, u32[]{:S(2)}) collective-permute-start(bf16[1,320,1024]{2,1,0:T(8,128)(2,1)S(1)} %fusion.57), channel_id=1, source_target_pairs={{1,0},{2,1},{3,2},{4,3},{5,4},{6,5},{7,6},{8,7},{9,8},{10,9},{11,1... | collective-permute-start | bytes 1966088 | tf_op jit(solution)/shard_map/ppermute | solution.py:19
  154.3 22.6 %collective-permute-start.7 = (bf16[1,320,1024]{2,1,0:T(8,128)(2,1)S(1)}, bf16[1,320,1024]{2,1,0:T(8,128)(2,1)}, u32[]{:S(2)}, u32[]{:S(2)}) collective-permute-start(bf16[1,320,1024]{2,1,0:T(8,128)(2,1)S(1)} %fusion.57), channel_id=1, source_target_pairs={{0,1},{1,2},{2,3},{3,4},{4,5},{5,6},{6,7},{7,8},{8,9},{9,10},{10,1... | collective-permute-start | bytes 1966088 | tf_op jit(solution)/shard_map/ppermute | solution.py:17
  180.8 14.9 %collective-permute-start.10 = (bf16[1,320,1024]{2,1,0:T(8,128)(2,1)}, bf16[1,320,1024]{2,1,0:T(8,128)(2,1)S(1)}, u32[]{:S(2)}, u32[]{:S(2)}) collective-permute-start(bf16[1,320,1024]{2,1,0:T(8,128)(2,1)} %fusion.46), channel_id=1, source_target_pairs={{0,64},{64,128},{128,192},{1,65},{65,129},{129,193},{2,66},{66,130... | collective-permute-start | bytes 1966088 | tf_op jit(solution)/shard_map/ppermute | solution.py:29
  182.7 40.6 %collective-permute-start.13 = (bf16[1,320,1024]{2,1,0:T(8,128)(2,1)S(1)}, bf16[1,320,1024]{2,1,0:T(8,128)(2,1)S(1)}, u32[]{:S(2)}, u32[]{:S(2)}) collective-permute-start(bf16[1,320,1024]{2,1,0:T(8,128)(2,1)S(1)} %get-tuple-element.19), channel_id=1, source_target_pairs={{0,64},{64,128},{128,192},{1,65},{65,129},{129,193},{2,66},{66,130... | collective-permute-start | bytes 1966088 | tf_op jit(solution)/shard_map/ppermute | solution.py:29
  197.3 30.4 %collective-permute-start.12 = (bf16[1,320,1024]{2,1,0:T(8,128)(2,1)S(1)}, bf16[1,320,1024]{2,1,0:T(8,128)(2,1)S(1)}, u32[]{:S(2)}, u32[]{:S(2)}) collective-permute-start(bf16[1,320,1024]{2,1,0:T(8,128)(2,1)S(1)} %fusion.60), channel_id=1, source_target_pairs={{1,0},{2,1},{3,2},{4,3},{5,4},{6,5},{7,6},{8,7},{9,8},{10,9},{11,1... | collective-permute-start | bytes 1966088 | tf_op jit(solution)/shard_map/ppermute | solution.py:19
  205.1 24.2 %collective-permute-start.11 = (bf16[1,320,1024]{2,1,0:T(8,128)(2,1)S(1)}, bf16[1,320,1024]{2,1,0:T(8,128)(2,1)}, u32[]{:S(2)}, u32[]{:S(2)}) collective-permute-start(bf16[1,320,1024]{2,1,0:T(8,128)(2,1)S(1)} %fusion.60), channel_id=1, source_target_pairs={{0,1},{1,2},{2,3},{3,4},{4,5},{5,6},{6,7},{7,8},{8,9},{9,10},{10,1... | collective-permute-start | bytes 1966088 | tf_op jit(solution)/shard_map/ppermute | solution.py:17
  232.8 3.9 copy-start.2
  232.8 20.9 %collective-permute-start.14 = (bf16[1,320,1024]{2,1,0:T(8,128)(2,1)S(1)}, bf16[1,320,1024]{2,1,0:T(8,128)(2,1)S(1)}, u32[]{:S(2)}, u32[]{:S(2)}) collective-permute-start(bf16[1,320,1024]{2,1,0:T(8,128)(2,1)S(1)} %fusion.45), channel_id=1, source_target_pairs={{0,64},{64,128},{128,192},{1,65},{65,129},{129,193},{2,66},{66,130... | collective-permute-start | bytes 1966088 | tf_op jit(solution)/shard_map/ppermute | solution.py:29
  234.7 39.6 %collective-permute-start.17 = (bf16[1,320,1024]{2,1,0:T(8,128)(2,1)S(1)}, bf16[1,320,1024]{2,1,0:T(8,128)(2,1)S(1)}, u32[]{:S(2)}, u32[]{:S(2)}) collective-permute-start(bf16[1,320,1024]{2,1,0:T(8,128)(2,1)S(1)} %get-tuple-element.17), channel_id=1, source_target_pairs={{0,64},{64,128},{128,192},{1,65},{65,129},{129,193},{2,66},{66,130... | collective-permute-start | bytes 1966088 | tf_op jit(solution)/shard_map/ppermute | solution.py:29
  254.1 23.5 %collective-permute-start.16 = (bf16[1,320,1024]{2,1,0:T(8,128)(2,1)S(1)}, bf16[1,320,1024]{2,1,0:T(8,128)(2,1)S(1)}, u32[]{:S(2)}, u32[]{:S(2)}) collective-permute-start(bf16[1,320,1024]{2,1,0:T(8,128)(2,1)S(1)} %fusion.63), channel_id=1, source_target_pairs={{1,0},{2,1},{3,2},{4,3},{5,4},{6,5},{7,6},{8,7},{9,8},{10,9},{11,1... | collective-permute-start | bytes 1966088 | tf_op jit(solution)/shard_map/ppermute | solution.py:19
  256.1 23.2 %collective-permute-start.15 = (bf16[1,320,1024]{2,1,0:T(8,128)(2,1)S(1)}, bf16[1,320,1024]{2,1,0:T(8,128)(2,1)}, u32[]{:S(2)}, u32[]{:S(2)}) collective-permute-start(bf16[1,320,1024]{2,1,0:T(8,128)(2,1)S(1)} %fusion.63), channel_id=1, source_target_pairs={{0,1},{1,2},{2,3},{3,4},{4,5},{5,6},{6,7},{7,8},{8,9},{9,10},{10,1... | collective-permute-start | bytes 1966088 | tf_op jit(solution)/shard_map/ppermute | solution.py:17
  283.1 14.0 %collective-permute-start.18 = (bf16[1,320,1024]{2,1,0:T(8,128)(2,1)}, bf16[1,320,1024]{2,1,0:T(8,128)(2,1)S(1)}, u32[]{:S(2)}, u32[]{:S(2)}) collective-permute-start(bf16[1,320,1024]{2,1,0:T(8,128)(2,1)} %fusion.44), channel_id=1, source_target_pairs={{0,64},{64,128},{128,192},{1,65},{65,129},{129,193},{2,66},{66,130... | collective-permute-start | bytes 1966088 | tf_op jit(solution)/shard_map/ppermute | solution.py:29
  285.1 31.5 %collective-permute-start.21 = (bf16[1,320,1024]{2,1,0:T(8,128)(2,1)S(1)}, bf16[1,320,1024]{2,1,0:T(8,128)(2,1)S(1)}, u32[]{:S(2)}, u32[]{:S(2)}) collective-permute-start(bf16[1,320,1024]{2,1,0:T(8,128)(2,1)S(1)} %get-tuple-element.15), channel_id=1, source_target_pairs={{0,64},{64,128},{128,192},{1,65},{65,129},{129,193},{2,66},{66,130... | collective-permute-start | bytes 1966088 | tf_op jit(solution)/shard_map/ppermute | solution.py:29
  297.6 26.2 %collective-permute-start.20 = (bf16[1,320,1024]{2,1,0:T(8,128)(2,1)S(1)}, bf16[1,320,1024]{2,1,0:T(8,128)(2,1)S(1)}, u32[]{:S(2)}, u32[]{:S(2)}) collective-permute-start(bf16[1,320,1024]{2,1,0:T(8,128)(2,1)S(1)} %fusion.66), channel_id=1, source_target_pairs={{1,0},{2,1},{3,2},{4,3},{5,4},{6,5},{7,6},{8,7},{9,8},{10,9},{11,1... | collective-permute-start | bytes 1966088 | tf_op jit(solution)/shard_map/ppermute | solution.py:19
  305.1 20.3 %collective-permute-start.19 = (bf16[1,320,1024]{2,1,0:T(8,128)(2,1)S(1)}, bf16[1,320,1024]{2,1,0:T(8,128)(2,1)}, u32[]{:S(2)}, u32[]{:S(2)}) collective-permute-start(bf16[1,320,1024]{2,1,0:T(8,128)(2,1)S(1)} %fusion.66), channel_id=1, source_target_pairs={{0,1},{1,2},{2,3},{3,4},{4,5},{5,6},{6,7},{7,8},{8,9},{9,10},{10,1... | collective-permute-start | bytes 1966088 | tf_op jit(solution)/shard_map/ppermute | solution.py:17
  328.9 33.3 %copy-start.3 = (bf16[1,320,1024]{2,1,0:T(8,128)(2,1)}, bf16[1,320,1024]{2,1,0:T(8,128)(2,1)S(1)}, u32[]{:S(2)}) copy-start(bf16[1,320,1024]{2,1,0:T(8,128)(2,1)S(1)} %fusion.43) | copy-start | bytes 1966084
  328.9 18.1 %collective-permute-start.22 = (bf16[1,320,1024]{2,1,0:T(8,128)(2,1)S(1)}, bf16[1,320,1024]{2,1,0:T(8,128)(2,1)S(1)}, u32[]{:S(2)}, u32[]{:S(2)}) collective-permute-start(bf16[1,320,1024]{2,1,0:T(8,128)(2,1)S(1)} %fusion.43), channel_id=1, source_target_pairs={{0,64},{64,128},{128,192},{1,65},{65,129},{129,193},{2,66},{66,130... | collective-permute-start | bytes 1966088 | tf_op jit(solution)/shard_map/ppermute | solution.py:29
  330.8 31.4 %collective-permute-start.25 = (bf16[1,320,1024]{2,1,0:T(8,128)(2,1)S(1)}, bf16[1,320,1024]{2,1,0:T(8,128)(2,1)S(1)}, u32[]{:S(2)}, u32[]{:S(2)}) collective-permute-start(bf16[1,320,1024]{2,1,0:T(8,128)(2,1)S(1)} %get-tuple-element.13), channel_id=1, source_target_pairs={{0,64},{64,128},{128,192},{1,65},{65,129},{129,193},{2,66},{66,130... | collective-permute-start | bytes 1966088 | tf_op jit(solution)/shard_map/ppermute | solution.py:29
  347.5 27.3 %collective-permute-start.24 = (bf16[1,320,1024]{2,1,0:T(8,128)(2,1)S(1)}, bf16[1,320,1024]{2,1,0:T(8,128)(2,1)S(1)}, u32[]{:S(2)}, u32[]{:S(2)}) collective-permute-start(bf16[1,320,1024]{2,1,0:T(8,128)(2,1)S(1)} %fusion.69), channel_id=1, source_target_pairs={{1,0},{2,1},{3,2},{4,3},{5,4},{6,5},{7,6},{8,7},{9,8},{10,9},{11,1... | collective-permute-start | bytes 1966088 | tf_op jit(solution)/shard_map/ppermute | solution.py:19
  356.9 19.7 %collective-permute-start.23 = (bf16[1,320,1024]{2,1,0:T(8,128)(2,1)S(1)}, bf16[1,320,1024]{2,1,0:T(8,128)(2,1)}, u32[]{:S(2)}, u32[]{:S(2)}) collective-permute-start(bf16[1,320,1024]{2,1,0:T(8,128)(2,1)S(1)} %fusion.69), channel_id=1, source_target_pairs={{0,1},{1,2},{2,3},{3,4},{4,5},{5,6},{6,7},{7,8},{8,9},{9,10},{10,1... | collective-permute-start | bytes 1966088 | tf_op jit(solution)/shard_map/ppermute | solution.py:17
Sparse Core Ops, SparseCore 0:
  9.2 32.4 all-gather.1
  383.7 59.1 reduce-scatter.1
where the time goes:
time: 455 us; the launch traced here: 450 us
  waiting for transfers between devices  273 us (60%)
  starting transfers between devices  88.5 us (19%)
  matrix products  60.9 us (13%)
  between operations  14 us (3%)
  other arithmetic  12.4 us (3%)
    ppermute x12, waiting for transfers between devices, shifted(): return lax.ppermute(array, axis, pairs)  148 us
    dot_general x28, matrix products, channel_mix(): jnp.einsum('io,fip->fop', weight, field, preferred_element_type=jnp.float32)  60.7 us
    reduce_scatter x1, waiting for transfers between devices, shards(): lax.psum_scatter(stacked.astype(jnp.bfloat16), 'segment', scatter_dimensi...  59.3 us
    ppermute x7, starting transfers between devices, extended(): lax.ppermute(head, axis, [((i + 1) % count, i) for i in range(ends)])  49.6 us
    ppermute x7, waiting for transfers between devices, extended(): lax.ppermute(head, axis, [((i + 1) % count, i) for i in range(ends)])  33.6 us
    all_gather x1, waiting for transfers between devices, shards(): all_clips = lax.all_gather(clips, 'segment', axis=0, tiled=True)  31.7 us
    ppermute x12, starting transfers between devices, shifted(): return lax.ppermute(array, axis, pairs)  23 us
    ppermute x7, starting transfers between devices, extended(): lax.ppermute(tail, axis, [(i, (i + 1) % count) for i in range(ends)])  15.9 us
  transfers between devices with their start and end apart: 28, of which 18 were waited for; matrix products, arithmetic and copies ran while one was open for 10% of the time, Pallas kernels for 0%

commit v1 on v0

v1 whole, which is shorter than its diff:
```python
import functools
import math

import jax
import jax.numpy as jnp
import numpy as np
from jax import lax
from jax.experimental import pallas as pl
from jax.experimental.pallas import tpu as pltpu
from jax.sharding import PartitionSpec as P

MESH = pl.DeviceIdType.MESH
LANES = 128
SECTIONS = 4
EMB_ROWS = 16


def unet_kernel(
    geometry,
    time_ref,
    freq_ref,
    gain_ref,
    taps_ref,
    film_ref,
    proj_ref,
    skip_ref,
    clips_ref,
    out_ref,
    raw,
    raw_skip,
    raw_film,
    wt,
    skt,
    film_rows,
    film_col,
    gain_col,
    state,
    nrm,
    halo_l,
    halo_r,
    load_sem,
    take_sem,
    swap_send,
    swap_recv,
    halo_send,
    halo_recv,
    own_send,
    own_recv,
    cut_send,
    cut_recv,
    side_send,
    side_recv,
    sib_send,
    sib_recv,
    film_send,
    film_recv,
    back_take,
    back_send,
    back_recv,
):
    C, chunks, frames, x_step, pieces = geometry
    half = pieces // 2
    rows = C // pieces
    half_pix = chunks * LANES
    groups = frames // 2
    f32, bf16 = jnp.float32, jnp.bfloat16

    seg = lax.axis_index("segment")
    frame = lax.axis_index("frame")
    y_hi, core = seg // 2, seg % 2
    group, y_lo = frame // 2, frame % 2
    x_par = (frame // x_step) % 2

    partner = (seg, group * 2 + 1 - y_lo)
    left = (seg, frame - 2)
    right = (seg, frame + 2)
    sibling = (y_hi * 2 + 1 - core, frame)
    across = ((1 - y_hi) * 2 + core, group * 2 + 1 - y_lo)
    beside = (seg, frame + x_step - 2 * x_step * x_par)
    has_left = group > 0
    has_right = group < groups - 1
    gathered = (1 - y_hi) * 2 + core
    relayed = (1 - y_hi) * 2 + 1 - core
    sib_own = y_hi * 2 + 1 - core

    def remote(src, dst, send, recv, device):
        return pltpu.make_async_remote_copy(
            src_ref=src, dst_ref=dst, send_sem=send, recv_sem=recv, device_id=device, device_id_type=MESH
        )

    loads = [
        pltpu.make_async_copy(taps_ref.at[0, 0], raw.at[pl.ds(0, C)], load_sem.at[0]),
        pltpu.make_async_copy(taps_ref.at[0, 1], raw.at[pl.ds(C, C)], load_sem.at[1]),
        pltpu.make_async_copy(taps_ref.at[0, 2], raw.at[pl.ds(2 * C, C)], load_sem.at[2]),
        pltpu.make_async_copy(proj_ref.at[0], raw.at[pl.ds(3 * C, C)], load_sem.at[3]),
        pltpu.make_async_copy(film_ref.at[0], raw_film, load_sem.at[4]),
        pltpu.make_async_copy(skip_ref.at[0], raw_skip.at[pl.ds(0, C)], load_sem.at[5]),
        pltpu.make_async_copy(skip_ref.at[1], raw_skip.at[pl.ds(C, C)], load_sem.at[6]),
    ]
    for load in loads:
        load.start()

    barrier = pltpu.get_barrier_semaphore()
    for device in (partner, sibling, across, beside):
        pl.semaphore_signal(barrier, inc=1, device_id=device, device_id_type=MESH)

    @pl.when(has_left)
    def _():
        pl.semaphore_signal(barrier, inc=1, device_id=left, device_id_type=MESH)

    @pl.when(has_right)
    def _():
        pl.semaphore_signal(barrier, inc=1, device_id=right, device_id_type=MESH)

    pl.semaphore_wait(barrier, 4 + has_left.astype(jnp.int32) + has_right.astype(jnp.int32))

    def pixels(part, c):
        return pl.ds(pl.multiple_of(part * half_pix + c * LANES, LANES), LANES)

    def swap(c):
        return remote(
            clips_ref.at[0, 0, :, pixels(1 - y_lo, c)],
            state.at[0, y_lo, c],
            swap_send.at[c],
            swap_recv.at[c],
            partner,
        )

    def take(c):
        return pltpu.make_async_copy(
            clips_ref.at[0, 0, :, pixels(y_lo, c)], state.at[0, y_lo, c], take_sem.at[c]
        )

    for c in range(chunks):
        swap(c).start()
        take(c).start()

    for load in loads[:4]:
        load.wait()
    for k in range(4 * C // LANES):
        wt[seg, :, k * LANES : (k + 1) * LANES] = raw[k * LANES : (k + 1) * LANES, :].T

    def own_piece(i):
        q = pl.ds(pl.multiple_of((x_par * half + i) * rows, 16), rows)
        return q

    to_sibling = remote(wt.at[seg], wt.at[seg], own_send.at[0], own_recv.at[0], sibling)
    from_sibling = remote(wt.at[sib_own], wt.at[sib_own], own_send.at[0], own_recv.at[0], sibling)
    to_sibling.start()

    def cut_out(i):
        q = own_piece(i)
        return remote(wt.at[seg, q], wt.at[seg, q], cut_send.at[i], cut_recv.at[i], across)

    def cut_in(i):
        q = own_piece(i)
        return remote(wt.at[gathered, q], wt.at[gathered, q], cut_send.at[i], cut_recv.at[i], across)

    def side_out(i):
        q = own_piece(i)
        return remote(wt.at[gathered, q], wt.at[gathered, q], side_send.at[i], side_recv.at[i], beside)

    def side_rows(i):
        return pl.ds(pl.multiple_of(((1 - x_par) * half + i) * rows, 16), rows)

    def side_in(i):
        q = side_rows(i)
        return remote(wt.at[gathered, q], wt.at[gathered, q], side_send.at[i], side_recv.at[i], beside)

    def sib_out(kind, i):
        q = own_piece(i) if kind == 0 else side_rows(i)
        return remote(wt.at[gathered, q], wt.at[gathered, q], sib_send.at[kind, i], sib_recv.at[kind, i], sibling)

    def sib_in(kind, i):
        q = own_piece(i) if kind == 0 else side_rows(i)
        return remote(wt.at[relayed, q], wt.at[relayed, q], sib_send.at[kind, i], sib_recv.at[kind, i], sibling)

    def forward(i):
        cut_in(i).wait_recv()
        side_out(i).start()
        sib_out(0, i).start()
        side_in(i).wait_recv()
        sib_out(1, i).start()

    def from_relay():
        for kind in range(2):
            for i in range(half):
                sib_in(kind, i).wait_recv()

    @pl.when(core == 0)
    def _():
        for i in range(half):
            cut_out(i).start()

    row = lax.broadcasted_iota(jnp.int32, (EMB_ROWS, 1), 0)
    when = jnp.zeros((EMB_ROWS, 1), jnp.int32)
    for m in range(SECTIONS):
        when = jnp.where(row == m, time_ref[m], when)
    angle = when.astype(f32) * freq_ref[...]
    lane = lax.broadcasted_iota(jnp.int32, angle.shape, 1)
    emb = jnp.where(lane < C // 2, jnp.sin(angle), jnp.cos(angle)).astype(bf16)
    loads[4].wait()
    film_rows[seg] = jnp.dot(emb, raw_film[...], preferred_element_type=f32)

    def film_copy(index, which, device):
        return remote(film_rows.at[index], film_rows.at[index], film_send.at[which], film_recv.at[which], device)

    film_copy(seg, 0, sibling).start()
    film_copy(seg, 1, across).start()

    def column(values):
        return jnp.broadcast_to(values, (LANES, C)).T

    for s in range(SECTIONS):
        gain_col[s] = column(gain_ref[s : s + 1, :])

    @pl.when(jnp.logical_not(has_left))
    def _():
        halo_l[...] = jnp.zeros_like(halo_l)

    @pl.when(jnp.logical_not(has_right))
    def _():
        halo_r[...] = jnp.zeros_like(halo_r)

    def to_left(s, c):
        return remote(nrm.at[s, 0, c], halo_r.at[s, c], halo_send.at[0, s, c], halo_recv.at[1, s, c], left)

    def to_right(s, c):
        return remote(nrm.at[s, 1, c], halo_l.at[s, c], halo_send.at[1, s, c], halo_recv.at[0, s, c], right)

    def normalize(values, s, c):
        meansq = jnp.sum(values * values, axis=0, keepdims=True) * (1.0 / C)
        scale = lax.rsqrt(meansq + 1e-05)
        gain = gain_col[s]
        nrm[s, 0, c] = (values[:, :LANES] * scale[:, :LANES] * gain).astype(bf16)
        nrm[s, 1, c] = (values[:, LANES:] * scale[:, LANES:] * gain).astype(bf16)

        @pl.when(has_left)
        def _():
            to_left(s, c).start()

        @pl.when(has_right)
        def _():
            to_right(s, c).start()

    def both(s, c):
        return jnp.concatenate([state[s, 0, c], state[s, 1, c]], axis=1)

    def first(c, carry):
        take(c).wait()
        swap_in = remote(
            clips_ref.at[0, 0, :, pixels(y_lo, c)],
            state.at[0, 1 - y_lo, c],
            swap_send.at[c],
            swap_recv.at[c],
            partner,
        )
        swap_in.wait_recv()
        normalize(both(0, c).astype(f32), 0, c)
        return carry

    lax.fori_loop(0, chunks, first, 0)

    @pl.when(core == 1)
    def _():
        for i in range(half):
            cut_out(i).start()

    for load in loads[5:]:
        load.wait()
    for n in range(2):
        for k in range(C // LANES + 1):
            lo, hi = k * LANES, min((k + 1) * LANES, C)
            skt[n, :, lo:hi] = raw_skip[n * C + lo : n * C + hi, :].T

    early = jnp.logical_and(y_hi == 1, core == 0)

    def pass_film():
        film_copy(gathered, 1, across).wait_recv()
        film_copy(gathered, 2, sibling).start()

    @pl.when(early)
    def _():
        pass_film()
        for i in range(half):
            forward(i)

    def back_own(c):
        return pltpu.make_async_copy(
            state.at[SECTIONS, y_lo, c], out_ref.at[0, 0, :, pixels(y_lo, c)], back_take.at[c]
        )

    def back_out(c):
        return remote(
            state.at[SECTIONS, 1 - y_lo, c],
            out_ref.at[0, 0, :, pixels(y_lo, c)],
            back_send.at[c],
            back_recv.at[c],
            partner,
        )

    def back_in(c):
        return remote(
            state.at[SECTIONS, 1 - y_lo, c],
            out_ref.at[0, 0, :, pixels(1 - y_lo, c)],
            back_send.at[c],
            back_recv.at[c],
            partner,
        )

    for s in range(SECTIONS):
        @pl.when(sib_own == s)
        def _():
            from_sibling.wait_recv()
            film_copy(sib_own, 0, sibling).wait_recv()

        @pl.when(relayed == s)
        def _():
            from_relay()
            film_copy(relayed, 2, sibling).wait_recv()

        mine = jnp.sum(jnp.where(row == seg, film_rows[s], 0.0), axis=0, keepdims=True)
        film_col[...] = column(1.0 + mine)

        def step(c, carry):
            @pl.when(has_left)
            def _():
                to_right(s, c).wait_recv()

            @pl.when(has_right)
            def _():
                to_left(s, c).wait_recv()

            n0, n1 = nrm[s, 0, c], nrm[s, 1, c]
            pad = jnp.zeros((4 * C - 3 * C - 2 * LANES, 2 * LANES), bf16)
            window = jnp.concatenate(
                [
                    jnp.concatenate([halo_l[s, c], n0], axis=1),
                    jnp.concatenate([n0, n1], axis=1),
                    jnp.concatenate([n1, halo_r[s, c]], axis=1),
                    pad,
                ],
                axis=0,
            )
            mixed = jnp.dot(wt[s, :, : 8 * LANES], window, preferred_element_type=f32)
            scale = film_col[...]
            hidden = jax.nn.silu(mixed * jnp.concatenate([scale, scale], axis=1)).astype(bf16)
            weights = wt[s, :, 7 * LANES :]
            fields = jnp.concatenate([pad, hidden], axis=0)
            if s == 2:
                weights = jnp.concatenate([weights, skt[0]], axis=1)
                fields = jnp.concatenate([fields, both(1, c)], axis=0)
            if s == 3:
                weights = jnp.concatenate([weights, skt[1]], axis=1)
                fields = jnp.concatenate([fields, both(0, c)], axis=0)
            total = both(s, c).astype(f32) + jnp.dot(weights, fields, preferred_element_type=f32)
            result = total.astype(bf16)
            state[s + 1, 0, c] = result[:, :LANES]
            state[s + 1, 1, c] = result[:, LANES:]
            if s + 1 < SECTIONS:
                normalize(result.astype(f32), s + 1, c)
            else:
                back_own(c).start()
                back_out(c).start()
            if s == 0:

                @pl.when(jnp.logical_not(early))
                def _():
                    forward(c)

            return carry

        lax.fori_loop(0, chunks, step, 0)
        if s == 0:

            @pl.when(jnp.logical_not(early))
            def _():
                for i in range(chunks, half):
                    forward(i)
                pass_film()

    def finish(c, carry):
        swap(c).wait_send()
        back_own(c).wait()
        back_out(c).wait_send()
        back_in(c).wait_recv()
        return carry

    lax.fori_loop(0, chunks, finish, 0)

    def sent(t, carry):
        s, c = t // chunks, t % chunks

        @pl.when(has_left)
        def _():
            to_left(s, c).wait_send()

        @pl.when(has_right)
        def _():
            to_right(s, c).wait_send()

        return carry

    lax.fori_loop(0, SECTIONS * chunks, sent, 0)
    to_sibling.wait_send()
    for i in range(half):
        cut_out(i).wait_send()
        side_out(i).wait_send()
        sib_out(0, i).wait_send()
        sib_out(1, i).wait_send()
    film_copy(seg, 0, sibling).wait_send()
    film_copy(seg, 1, across).wait_send()
    film_copy(gathered, 2, sibling).wait_send()


def shards(geometry, clips, timesteps, gain, temporal_weight, film_weight, out_weight, skip_weight):
    C, chunks, frames, x_step, pieces = geometry
    half = pieces // 2
    base = np.exp(-math.log(10000.0) * np.arange(C // 2) / (C // 2))
    freq = jnp.asarray(np.concatenate([base, base])[None, :].astype(np.float32))
    vmem = pl.BlockSpec(memory_space=pltpu.VMEM)
    any_space = pl.BlockSpec(memory_space=pl.ANY)
    bf16, f32 = jnp.bfloat16, jnp.float32
    dma = pltpu.SemaphoreType.DMA
    flops = 2 * 18 * C * C * 2 * chunks * LANES
    return pl.pallas_call(
        functools.partial(unet_kernel, geometry),
        out_shape=jax.ShapeDtypeStruct(clips.shape, bf16),
        in_specs=[
            pl.BlockSpec(memory_space=pltpu.SMEM),
            vmem,
            vmem,
            any_space,
            any_space,
            any_space,
            any_space,
            any_space,
        ],
        out_specs=any_space,
        scratch_shapes=[
            pltpu.VMEM((4 * C, C), bf16),
            pltpu.VMEM((2 * C, C), bf16),
            pltpu.VMEM((C, C), bf16),
            pltpu.VMEM((SECTIONS, C, 4 * C), bf16),
            pltpu.VMEM((2, C, C), bf16),
            pltpu.VMEM((SECTIONS, EMB_ROWS, C), f32),
            pltpu.VMEM((C, LANES), f32),
            pltpu.VMEM((SECTIONS, C, LANES), f32),
            pltpu.VMEM((SECTIONS + 1, 2, chunks, C, LANES), bf16),
            pltpu.VMEM((SECTIONS, 2, chunks, C, LANES), bf16),
            pltpu.VMEM((SECTIONS, chunks, C, LANES), bf16),
            pltpu.VMEM((SECTIONS, chunks, C, LANES), bf16),
            dma((7,)),
            dma((chunks,)),
            dma((chunks,)),
            dma((chunks,)),
            dma((2, SECTIONS, chunks)),
            dma((2, SECTIONS, chunks)),
            dma((1,)),
            dma((1,)),
            dma((half,)),
            dma((half,)),
            dma((half,)),
            dma((half,)),
            dma((2, half)),
            dma((2, half)),
            dma((3,)),
            dma((3,)),
            dma((chunks,)),
            dma((chunks,)),
            dma((chunks,)),
        ],
        compiler_params=pltpu.CompilerParams(
            collective_id=0, has_side_effects=True, vmem_limit_bytes=48 * 2**20
        ),
        cost_estimate=pl.CostEstimate(flops=flops, bytes_accessed=4 * clips.size, transcendentals=0),
        name="unet",
    )(timesteps, freq, gain, temporal_weight, film_weight, out_weight, skip_weight, clips)


def solution(mesh):
    frames = mesh.shape["frame"]

    def run(clips, *rest):
        _, _, C, pix = clips.shape
        x_step = 16 if frames >= 32 else 2
        geometry = (C, pix // 2 // LANES, frames, x_step, C // 32)
        return shards(geometry, clips, *rest)

    placed = (
        P("segment", "frame", None, None),
        P(),
        P(),
        P("segment", None, None, None),
        P("segment", None, None),
        P("segment", None, None),
        P(),
    )
    return jax.shard_map(
        run,
        mesh=mesh,
        in_specs=placed,
        out_specs=P("segment", "frame", None, None),
        check_vma=False,
    )
```

time: 455 us -> 89 us (0.20)
  the two profiles are of different devices: /device:TPU:18 before, /device:TPU:20 now
where the time goes in v1:
time: 89 us; the launch traced here: 88.7 us
  Pallas kernels  80.7 us (91%)
  local copies, waits for them, and re-layouts  7.98 us (9%)
    pallas_call x1, Pallas kernels, shards(): pl.pallas_call(functools.partial(unet_kernel, geometry), out_shape=jax.Sh...  80.7 us
    unnamed x17, local copies, waits for them, and re-layouts  7.98 us

profile of v1, /device:TPU:20, one launch (start us, length us, event | category | flops | bytes accessed | tf_op | source)
XLA Modules:
  0.0 88.7 jit_solution(10307646751086711419)
XLA Ops:
  0.0 0.0 copy-start
  0.0 1.1 %copy-done = bf16[1,3,320,320]{3,2,1,0:T(8,128)(2,1)S(1)} copy-done((bf16[1,3,320,320]{3,2,1,0:T(8,128)(2,1)S(1)}, bf16[1,3,320,320]{3,2,1,0:T(8,128)(2,1)}, u32[]{:S(2)}) %copy-start) | copy-done | bytes 614424
  1.1 0.0 copy-start.1
  1.1 1.1 %copy-done.1 = bf16[1,1,320,1024]{3,2,1,0:T(8,128)(2,1)S(1)} copy-done((bf16[1,1,320,1024]{3,2,1,0:T(8,128)(2,1)S(1)}, bf16[1,1,320,1024]{3,2,1,0:T(8,128)(2,1)}, u32[]{:S(2)}) %copy-start.1) | copy-done | bytes 655384
  2.2 0.0 copy-start.2
  2.2 1.0 %copy-done.2 = bf16[2,320,320]{2,1,0:T(8,128)(2,1)S(1)} copy-done((bf16[2,320,320]{2,1,0:T(8,128)(2,1)S(1)}, bf16[2,320,320]{2,1,0:T(8,128)(2,1)}, u32[]{:S(2)}) %copy-start.2) | copy-done | bytes 409624
  3.2 0.0 copy-start.3
  3.2 0.9 %copy-done.3 = bf16[1,320,320]{2,1,0:T(8,128)(2,1)S(1)} copy-done((bf16[1,320,320]{2,1,0:T(8,128)(2,1)S(1)}, bf16[1,320,320]{2,1,0:T(8,128)(2,1)}, u32[]{:S(2)}) %copy-start.3) | copy-done | bytes 204824
  4.2 0.0 copy-start.4
  4.2 0.9 %copy-done.4 = bf16[1,320,320]{2,1,0:T(8,128)(2,1)S(1)} copy-done((bf16[1,320,320]{2,1,0:T(8,128)(2,1)S(1)}, bf16[1,320,320]{2,1,0:T(8,128)(2,1)}, u32[]{:S(2)}) %copy-start.4) | copy-done | bytes 204824
  5.1 0.0 copy-start.5
  5.1 0.7 copy-done.5
  5.8 0.0 copy-start.6
  5.8 0.7 copy-done.6
  6.5 0.0 copy-start.7
  6.5 0.7 copy-done.7
  7.2 80.7 %unet.1 = bf16[1,1,320,1024]{3,2,1,0:T(8,128)(2,1)S(1)} custom-call(s32[4]{0:T(128)S(1)} %copy-done.6, f32[1,320]{1,0:T(1,128)S(1)} %copy-done.7, f32[4,320]{1,0:T(4,128)S(1)} %copy-done.5, bf16[1,3,320,320]{3,2,1,0:T(8,128)(2,1)S(1)} %copy-done, bf16[1,320,320]{2,1,0:T(8,128)(2,1)S(1)} %copy-done.3, bf16[1,320,320]{2,1,0:T(8,128)(2,1)S(1)} %copy-done.4, ...), custom_call_target="tpu_custom_call" | custom-call | flops 3774873600 | bytes 1310720 | tf_op jit(solution)/shard_map/unet/pallas_call | solution.py:426
  87.8 0.8 copy.10
Async XLA Ops:
  0.0 1.1 %copy-start = (bf16[1,3,320,320]{3,2,1,0:T(8,128)(2,1)S(1)}, bf16[1,3,320,320]{3,2,1,0:T(8,128)(2,1)}, u32[]{:S(2)}) copy-start(bf16[1,3,320,320]{3,2,1,0:T(8,128)(2,1)} %taps_ref.1) | copy-start | bytes 1843204
  1.1 1.1 %copy-start.1 = (bf16[1,1,320,1024]{3,2,1,0:T(8,128)(2,1)S(1)}, bf16[1,1,320,1024]{3,2,1,0:T(8,128)(2,1)}, u32[]{:S(2)}) copy-start(bf16[1,1,320,1024]{3,2,1,0:T(8,128)(2,1)} %clips_ref.1) | copy-start | bytes 1966084
  2.2 1.0 %copy-start.2 = (bf16[2,320,320]{2,1,0:T(8,128)(2,1)S(1)}, bf16[2,320,320]{2,1,0:T(8,128)(2,1)}, u32[]{:S(2)}) copy-start(bf16[2,320,320]{2,1,0:T(8,128)(2,1)} %skip_ref.1) | copy-start | bytes 1228804
  3.2 0.9 %copy-start.3 = (bf16[1,320,320]{2,1,0:T(8,128)(2,1)S(1)}, bf16[1,320,320]{2,1,0:T(8,128)(2,1)}, u32[]{:S(2)}) copy-start(bf16[1,320,320]{2,1,0:T(8,128)(2,1)} %film_ref.1) | copy-start | bytes 614404
  4.2 0.9 %copy-start.4 = (bf16[1,320,320]{2,1,0:T(8,128)(2,1)S(1)}, bf16[1,320,320]{2,1,0:T(8,128)(2,1)}, u32[]{:S(2)}) copy-start(bf16[1,320,320]{2,1,0:T(8,128)(2,1)} %proj_ref.1) | copy-start | bytes 614404
  5.1 0.7 copy-start.5
  5.8 0.7 copy-start.6
  6.5 0.7 copy-start.7

commit v2 on v1

--- a/solution.py
+++ b/solution.py
@@ -12,7 +12,7 @@
 MESH = pl.DeviceIdType.MESH
 LANES = 128
 SECTIONS = 4
-EMB_ROWS = 16
+EMB_ROWS = 8
 
 
 def unet_kernel(
@@ -26,6 +26,9 @@
     skip_ref,
     clips_ref,
     out_ref,
+    time_smem,
+    freq_vmem,
+    gain_vmem,
     raw,
     raw_skip,
     raw_film,
@@ -58,9 +61,9 @@
     back_send,
     back_recv,
 ):
-    C, chunks, frames, x_step, pieces = geometry
+    C, chunks, frames = geometry
+    pieces = 4 * C // LANES
     half = pieces // 2
-    rows = C // pieces
     half_pix = chunks * LANES
     groups = frames // 2
     f32, bf16 = jnp.float32, jnp.bfloat16
@@ -69,14 +72,12 @@
     frame = lax.axis_index("frame")
     y_hi, core = seg // 2, seg % 2
     group, y_lo = frame // 2, frame % 2
-    x_par = (frame // x_step) % 2
 
     partner = (seg, group * 2 + 1 - y_lo)
     left = (seg, frame - 2)
     right = (seg, frame + 2)
     sibling = (y_hi * 2 + 1 - core, frame)
     across = ((1 - y_hi) * 2 + core, group * 2 + 1 - y_lo)
-    beside = (seg, frame + x_step - 2 * x_step * x_par)
     has_left = group > 0
     has_right = group < groups - 1
     gathered = (1 - y_hi) * 2 + core
@@ -96,26 +97,42 @@
         pltpu.make_async_copy(film_ref.at[0], raw_film, load_sem.at[4]),
         pltpu.make_async_copy(skip_ref.at[0], raw_skip.at[pl.ds(0, C)], load_sem.at[5]),
         pltpu.make_async_copy(skip_ref.at[1], raw_skip.at[pl.ds(C, C)], load_sem.at[6]),
+        pltpu.make_async_copy(time_ref, time_smem, load_sem.at[7]),
+        pltpu.make_async_copy(freq_ref, freq_vmem, load_sem.at[8]),
+        pltpu.make_async_copy(gain_ref, gain_vmem, load_sem.at[9]),
     ]
     for load in loads:
         load.start()
 
-    barrier = pltpu.get_barrier_semaphore()
-    for device in (partner, sibling, across, beside):
-        pl.semaphore_signal(barrier, inc=1, device_id=device, device_id_type=MESH)
-
-    @pl.when(has_left)
-    def _():
-        pl.semaphore_signal(barrier, inc=1, device_id=left, device_id_type=MESH)
-
-    @pl.when(has_right)
-    def _():
-        pl.semaphore_signal(barrier, inc=1, device_id=right, device_id_type=MESH)
-
-    pl.semaphore_wait(barrier, 4 + has_left.astype(jnp.int32) + has_right.astype(jnp.int32))
-
     def pixels(part, c):
         return pl.ds(pl.multiple_of(part * half_pix + c * LANES, LANES), LANES)
+
+    def take(c):
+        return pltpu.make_async_copy(
+            clips_ref.at[0, 0, :, pixels(y_lo, c)], state.at[0, y_lo, c], take_sem.at[c]
+        )
+
+    for c in range(chunks):
+        take(c).start()
+
+    barrier = pltpu.get_barrier_semaphore()
+    for device in (partner, sibling, across):
+        pl.semaphore_signal(barrier, inc=1, device_id=device, device_id_type=MESH)
+
+    @pl.when(has_left)
+    def _():
+        pl.semaphore_signal(barrier, inc=1, device_id=left, device_id_type=MESH)
+
+    @pl.when(has_right)
+    def _():
+        pl.semaphore_signal(barrier, inc=1, device_id=right, device_id_type=MESH)
+
+    for load in loads[:4]:
+        load.wait()
+    for k in range(pieces):
+        wt[seg, :, k * LANES : (k + 1) * LANES] = raw[k * LANES : (k + 1) * LANES, :].T
+
+    pl.semaphore_wait(barrier, 3 + has_left.astype(jnp.int32) + has_right.astype(jnp.int32))
 
     def swap(c):
         return remote(
@@ -126,77 +143,56 @@
             partner,
         )
 
-    def take(c):
-        return pltpu.make_async_copy(
-            clips_ref.at[0, 0, :, pixels(y_lo, c)], state.at[0, y_lo, c], take_sem.at[c]
-        )
-
     for c in range(chunks):
         swap(c).start()
-        take(c).start()
-
-    for load in loads[:4]:
+
+    early = jnp.logical_and(y_hi == 1, core == 0)
+    first_source = jnp.logical_and(y_hi == 0, core == 0)
+
+    def block(index, q):
+        return wt.at[index, :, pl.ds(pl.multiple_of(q * LANES, LANES), LANES)]
+
+    def own_to_sibling(index):
+        return remote(wt.at[index], wt.at[index], own_send.at[0], own_recv.at[0], sibling)
+
+    def to_across(index, q):
+        return remote(block(index, q), block(index, q), cut_send.at[q], cut_recv.at[q], across)
+
+    def to_partner(index, q):
+        return remote(block(index, q), block(index, q), side_send.at[q], side_recv.at[q], partner)
+
+    def to_sibling(index, q):
+        return remote(block(index, q), block(index, q), sib_send.at[q], sib_recv.at[q], sibling)
+
+    def forward_all(q):
+        to_across(gathered, q).wait_recv()
+        to_sibling(gathered, q).start()
+
+    def forward_cut(i):
+        q = 2 * i + y_lo
+        to_across(gathered, q).wait_recv()
+        to_partner(gathered, q).start()
+        to_sibling(gathered, q).start()
+
+    def forward_side(i):
+        q = 2 * i + 1 - y_lo
+        to_partner(gathered, q).wait_recv()
+        to_sibling(gathered, q).start()
+
+    @pl.when(first_source)
+    def _():
+        for q in range(pieces):
+            to_across(seg, q).start()
+
+    own_to_sibling(seg).start()
+
+    for load in loads[7:]:
         load.wait()
-    for k in range(4 * C // LANES):
-        wt[seg, :, k * LANES : (k + 1) * LANES] = raw[k * LANES : (k + 1) * LANES, :].T
-
-    def own_piece(i):
-        q = pl.ds(pl.multiple_of((x_par * half + i) * rows, 16), rows)
-        return q
-
-    to_sibling = remote(wt.at[seg], wt.at[seg], own_send.at[0], own_recv.at[0], sibling)
-    from_sibling = remote(wt.at[sib_own], wt.at[sib_own], own_send.at[0], own_recv.at[0], sibling)
-    to_sibling.start()
-
-    def cut_out(i):
-        q = own_piece(i)
-        return remote(wt.at[seg, q], wt.at[seg, q], cut_send.at[i], cut_recv.at[i], across)
-
-    def cut_in(i):
-        q = own_piece(i)
-        return remote(wt.at[gathered, q], wt.at[gathered, q], cut_send.at[i], cut_recv.at[i], across)
-
-    def side_out(i):
-        q = own_piece(i)
-        return remote(wt.at[gathered, q], wt.at[gathered, q], side_send.at[i], side_recv.at[i], beside)
-
-    def side_rows(i):
-        return pl.ds(pl.multiple_of(((1 - x_par) * half + i) * rows, 16), rows)
-
-    def side_in(i):
-        q = side_rows(i)
-        return remote(wt.at[gathered, q], wt.at[gathered, q], side_send.at[i], side_recv.at[i], beside)
-
-    def sib_out(kind, i):
-        q = own_piece(i) if kind == 0 else side_rows(i)
-        return remote(wt.at[gathered, q], wt.at[gathered, q], sib_send.at[kind, i], sib_recv.at[kind, i], sibling)
-
-    def sib_in(kind, i):
-        q = own_piece(i) if kind == 0 else side_rows(i)
-        return remote(wt.at[relayed, q], wt.at[relayed, q], sib_send.at[kind, i], sib_recv.at[kind, i], sibling)
-
-    def forward(i):
-        cut_in(i).wait_recv()
-        side_out(i).start()
-        sib_out(0, i).start()
-        side_in(i).wait_recv()
-        sib_out(1, i).start()
-
-    def from_relay():
-        for kind in range(2):
-            for i in range(half):
-                sib_in(kind, i).wait_recv()
-
-    @pl.when(core == 0)
-    def _():
-        for i in range(half):
-            cut_out(i).start()
-
     row = lax.broadcasted_iota(jnp.int32, (EMB_ROWS, 1), 0)
     when = jnp.zeros((EMB_ROWS, 1), jnp.int32)
     for m in range(SECTIONS):
-        when = jnp.where(row == m, time_ref[m], when)
-    angle = when.astype(f32) * freq_ref[...]
+        when = jnp.where(row == m, time_smem[m], when)
+    angle = when.astype(f32) * freq_vmem[...]
     lane = lax.broadcasted_iota(jnp.int32, angle.shape, 1)
     emb = jnp.where(lane < C // 2, jnp.sin(angle), jnp.cos(angle)).astype(bf16)
     loads[4].wait()
@@ -212,7 +208,7 @@
         return jnp.broadcast_to(values, (LANES, C)).T
 
     for s in range(SECTIONS):
-        gain_col[s] = column(gain_ref[s : s + 1, :])
+        gain_col[s] = column(gain_vmem[s : s + 1, :])
 
     @pl.when(jnp.logical_not(has_left))
     def _():
@@ -257,23 +253,27 @@
         )
         swap_in.wait_recv()
         normalize(both(0, c).astype(f32), 0, c)
+
+        @pl.when(early)
+        def _():
+            forward_all(2 * c)
+            forward_all(2 * c + 1)
+
         return carry
 
-    lax.fori_loop(0, chunks, first, 0)
-
-    @pl.when(core == 1)
-    def _():
-        for i in range(half):
-            cut_out(i).start()
-
-    for load in loads[5:]:
+    for load in loads[5:7]:
         load.wait()
     for n in range(2):
         for k in range(C // LANES + 1):
             lo, hi = k * LANES, min((k + 1) * LANES, C)
             skt[n, :, lo:hi] = raw_skip[n * C + lo : n * C + hi, :].T
 
-    early = jnp.logical_and(y_hi == 1, core == 0)
+    lax.fori_loop(0, chunks, first, 0)
+
+    @pl.when(jnp.logical_not(first_source))
+    def _():
+        for i in range(half):
+            to_across(seg, 2 * i + 1 - y_lo).start()
 
     def pass_film():
         film_copy(gathered, 1, across).wait_recv()
@@ -281,9 +281,9 @@
 
     @pl.when(early)
     def _():
+        for q in range(min(2 * chunks, pieces), pieces):
+            forward_all(q)
         pass_film()
-        for i in range(half):
-            forward(i)
 
     def back_own(c):
         return pltpu.make_async_copy(
@@ -311,12 +311,13 @@
     for s in range(SECTIONS):
         @pl.when(sib_own == s)
         def _():
-            from_sibling.wait_recv()
+            own_to_sibling(sib_own).wait_recv()
             film_copy(sib_own, 0, sibling).wait_recv()
 
         @pl.when(relayed == s)
         def _():
-            from_relay()
+            for q in range(pieces):
+                to_sibling(relayed, q).wait_recv()
             film_copy(relayed, 2, sibling).wait_recv()
 
         mine = jnp.sum(jnp.where(row == seg, film_rows[s], 0.0), axis=0, keepdims=True)
@@ -366,7 +367,11 @@
 
                 @pl.when(jnp.logical_not(early))
                 def _():
-                    forward(c)
+                    forward_cut(c)
+
+                    @pl.when(c >= 2)
+                    def _():
+                        forward_side(c - 2)
 
             return carry
 
@@ -376,7 +381,9 @@
             @pl.when(jnp.logical_not(early))
             def _():
                 for i in range(chunks, half):
-                    forward(i)
+                    forward_cut(i)
+                for i in range(max(chunks - 2, 0), half):
+                    forward_side(i)
                 pass_film()
 
     def finish(c, carry):
@@ -402,42 +409,48 @@
         return carry
 
     lax.fori_loop(0, SECTIONS * chunks, sent, 0)
-    to_sibling.wait_send()
-    for i in range(half):
-        cut_out(i).wait_send()
-        side_out(i).wait_send()
-        sib_out(0, i).wait_send()
-        sib_out(1, i).wait_send()
+    own_to_sibling(seg).wait_send()
+
+    @pl.when(first_source)
+    def _():
+        for q in range(pieces):
+            to_across(seg, q).wait_send()
+
+    @pl.when(jnp.logical_not(first_source))
+    def _():
+        for i in range(half):
+            to_across(seg, 2 * i + 1 - y_lo).wait_send()
+
+    @pl.when(jnp.logical_not(early))
+    def _():
+        for i in range(half):
+            to_partner(gathered, 2 * i + y_lo).wait_send()
+
+    for q in range(pieces):
+        to_sibling(gathered, q).wait_send()
     film_copy(seg, 0, sibling).wait_send()
     film_copy(seg, 1, across).wait_send()
     film_copy(gathered, 2, sibling).wait_send()
 
 
 def shards(geometry, clips, timesteps, gain, temporal_weight, film_weight, out_weight, skip_weight):
-    C, chunks, frames, x_step, pieces = geometry
-    half = pieces // 2
+    C, chunks, frames = geometry
+    pieces = 4 * C // LANES
     base = np.exp(-math.log(10000.0) * np.arange(C // 2) / (C // 2))
     freq = jnp.asarray(np.concatenate([base, base])[None, :].astype(np.float32))
-    vmem = pl.BlockSpec(memory_space=pltpu.VMEM)
-    any_space = pl.BlockSpec(memory_space=pl.ANY)
+    hbm = pl.BlockSpec(memory_space=pltpu.HBM)
     bf16, f32 = jnp.bfloat16, jnp.float32
     dma = pltpu.SemaphoreType.DMA
     flops = 2 * 18 * C * C * 2 * chunks * LANES
     return pl.pallas_call(
         functools.partial(unet_kernel, geometry),
         out_shape=jax.ShapeDtypeStruct(clips.shape, bf16),
-        in_specs=[
-            pl.BlockSpec(memory_space=pltpu.SMEM),
-            vmem,
-            vmem,
-            any_space,
-            any_space,
-            any_space,
-            any_space,
-            any_space,
-        ],
-        out_specs=any_space,
+        in_specs=[hbm] * 8,
+        out_specs=hbm,
         scratch_shapes=[
+            pltpu.SMEM(timesteps.shape, jnp.int32),
+            pltpu.VMEM(freq.shape, f32),
+            pltpu.VMEM(gain.shape, f32),
             pltpu.VMEM((4 * C, C), bf16),
             pltpu.VMEM((2 * C, C), bf16),
             pltpu.VMEM((C, C), bf16),
@@ -450,7 +463,7 @@
             pltpu.VMEM((SECTIONS, 2, chunks, C, LANES), bf16),
             pltpu.VMEM((SECTIONS, chunks, C, LANES), bf16),
             pltpu.VMEM((SECTIONS, chunks, C, LANES), bf16),
-            dma((7,)),
+            dma((10,)),
             dma((chunks,)),
             dma((chunks,)),
             dma((chunks,)),
@@ -458,12 +471,12 @@
             dma((2, SECTIONS, chunks)),
             dma((1,)),
             dma((1,)),
-            dma((half,)),
-            dma((half,)),
-            dma((half,)),
-            dma((half,)),
-            dma((2, half)),
-            dma((2, half)),
+            dma((pieces,)),
+            dma((pieces,)),
+            dma((pieces,)),
+            dma((pieces,)),
+            dma((pieces,)),
+            dma((pieces,)),
             dma((3,)),
             dma((3,)),
             dma((chunks,)),
@@ -471,7 +484,7 @@
             dma((chunks,)),
         ],
         compiler_params=pltpu.CompilerParams(
-            collective_id=0, has_side_effects=True, vmem_limit_bytes=48 * 2**20
+            collective_id=0, has_side_effects=True, vmem_limit_bytes=63 * 2**20
         ),
         cost_estimate=pl.CostEstimate(flops=flops, bytes_accessed=4 * clips.size, transcendentals=0),
         name="unet",
@@ -483,8 +496,7 @@
 
     def run(clips, *rest):
         _, _, C, pix = clips.shape
-        x_step = 16 if frames >= 32 else 2
-        geometry = (C, pix // 2 // LANES, frames, x_step, C // 32)
+        geometry = (C, pix // 2 // LANES, frames)
         return shards(geometry, clips, *rest)
 
     placed = (

time: 89 us -> 56 us (0.63)
  the two profiles are of different devices: /device:TPU:20 before, /device:TPU:18 now
where the time goes in v2:
time: 56 us; the launch traced here: 55.5 us
  Pallas kernels  53.6 us (96%)
  local copies, waits for them, and re-layouts  1.97 us (4%)
    pallas_call x1, Pallas kernels, shards(): pl.pallas_call(functools.partial(unet_kernel, geometry), out_shape=jax.Sh...  53.6 us
    unnamed x1, local copies, waits for them, and re-layouts  1.97 us

profile of v2, /device:TPU:18, one launch (start us, length us, event | category | flops | bytes accessed | tf_op | source)
XLA Modules:
  0.0 55.5 jit_solution(4085773912306710534)
XLA Ops:
  0.0 53.6 %unet.1 = bf16[1,1,320,1024]{3,2,1,0:T(8,128)(2,1)} custom-call(s32[4]{0:T(128)} %time_ref.1, f32[1,320]{1,0:T(1,128)} %constant.2.clone.freq_ref, f32[4,320]{1,0:T(4,128)} %gain_ref.1, bf16[1,3,320,320]{3,2,1,0:T(8,128)(2,1)} %taps_ref.1, bf16[1,320,320]{2,1,0:T(8,128)(2,1)} %film_ref.1, bf16[1,320,320]{2,1,0:T(8,128)(2,1)} %proj_ref.1, ...), custom_call_target="tpu_custom_call" | custom-call | flops 3774873600 | bytes 1310720 | tf_op jit(solution)/shard_map/unet/pallas_call | solution.py:445
  53.6 2.0 %copy.10 = bf16[1,1,320,1024]{3,2,1,0:T(8,128)(2,1)} copy(bf16[1,1,320,1024]{3,2,1,0:T(8,128)(2,1)} %unet.1) | data formatting | bytes 1310720

commit v3 on v2

v3 whole, which is shorter than its diff:
```python
import functools
import math

import jax
import jax.numpy as jnp
import numpy as np
from jax import lax
from jax.experimental import pallas as pl
from jax.experimental.pallas import tpu as pltpu
from jax.sharding import PartitionSpec as P

MESH = pl.DeviceIdType.MESH
LANES = 128
SECTIONS = 4
EMB_ROWS = 8


def unet_kernel(
    geometry,
    time_ref,
    freq_ref,
    gain_ref,
    taps_ref,
    film_ref,
    proj_ref,
    skip_ref,
    clips_ref,
    out_ref,
    time_smem,
    freq_vmem,
    gain_vmem,
    raw,
    raw_skip,
    raw_film,
    wt,
    skt,
    film_rows,
    film_col,
    gain_col,
    window,
    norm0,
    norm1,
    state,
    nrm,
    halo_l,
    halo_r,
    give,
    load_sem,
    take_sem,
    swap_send,
    swap_recv,
    deep_send,
    deep_recv,
    halo_send,
    halo_recv,
    own_send,
    own_recv,
    cut_send,
    cut_recv,
    side_send,
    side_recv,
    sib_send,
    sib_recv,
    film_send,
    film_recv,
    back_send,
    back_recv,
):
    C, chunks, frames = geometry
    pieces = 4 * C // LANES
    half = pieces // 2
    half_pix = chunks * LANES
    groups = frames // 2
    f32, bf16 = jnp.float32, jnp.bfloat16

    seg = lax.axis_index("segment")
    frame = lax.axis_index("frame")
    y_hi, core = seg // 2, seg % 2
    group, y_lo = frame // 2, frame % 2

    partner = (seg, group * 2 + 1 - y_lo)
    left = (seg, frame - 2)
    right = (seg, frame + 2)
    sibling = (y_hi * 2 + 1 - core, frame)
    across = ((1 - y_hi) * 2 + core, group * 2 + 1 - y_lo)
    has_left = group > 0
    has_right = group < groups - 1
    gathered = (1 - y_hi) * 2 + core
    relayed = (1 - y_hi) * 2 + 1 - core
    sib_own = y_hi * 2 + 1 - core
    early = jnp.logical_and(y_hi == 1, core == 0)
    second = jnp.logical_and(y_hi == 1, core == 1)
    patient = jnp.logical_and(y_hi == 0, core == 1)

    def remote(src, dst, send, recv, device):
        return pltpu.make_async_remote_copy(
            src_ref=src, dst_ref=dst, send_sem=send, recv_sem=recv, device_id=device, device_id_type=MESH
        )

    def at_left(action):
        pl.when(has_left)(action)

    def at_right(action):
        pl.when(has_right)(action)

    loads = [
        pltpu.make_async_copy(taps_ref.at[0, 0], raw.at[pl.ds(0, C)], load_sem.at[0]),
        pltpu.make_async_copy(taps_ref.at[0, 1], raw.at[pl.ds(C, C)], load_sem.at[1]),
        pltpu.make_async_copy(taps_ref.at[0, 2], raw.at[pl.ds(2 * C, C)], load_sem.at[2]),
        pltpu.make_async_copy(proj_ref.at[0], raw.at[pl.ds(3 * C, C)], load_sem.at[3]),
        pltpu.make_async_copy(film_ref.at[0], raw_film, load_sem.at[4]),
        pltpu.make_async_copy(skip_ref.at[0], raw_skip.at[pl.ds(0, C)], load_sem.at[5]),
        pltpu.make_async_copy(skip_ref.at[1], raw_skip.at[pl.ds(C, C)], load_sem.at[6]),
        pltpu.make_async_copy(time_ref, time_smem, load_sem.at[7]),
        pltpu.make_async_copy(freq_ref, freq_vmem, load_sem.at[8]),
        pltpu.make_async_copy(gain_ref, gain_vmem, load_sem.at[9]),
    ]
    for load in loads[:4]:
        load.start()

    def pixels(part, c):
        return pl.ds(pl.multiple_of(part * half_pix + c * LANES, LANES), LANES)

    def take(c):
        return pltpu.make_async_copy(
            clips_ref.at[0, 0, :, pixels(y_lo, c)], window.at[2 + y_lo, c], take_sem.at[c]
        )

    for c in range(chunks):
        take(c).start()
    for load in loads[4:]:
        load.start()

    barrier = pltpu.get_barrier_semaphore()
    at_left(lambda: pl.semaphore_signal(barrier, inc=1, device_id=left, device_id_type=MESH))
    at_right(lambda: pl.semaphore_signal(barrier, inc=1, device_id=right, device_id_type=MESH))
    for device in (partner, sibling, across):
        pl.semaphore_signal(barrier, inc=1, device_id=device, device_id_type=MESH)

    def turn():
        for load in loads[:4]:
            load.wait()
        for k in range(pieces):
            wt[seg, :, k * LANES : (k + 1) * LANES] = raw[k * LANES : (k + 1) * LANES, :].T

    source = jnp.logical_and(y_hi == 0, core == 0)
    pl.when(source)(turn)

    pl.semaphore_wait(barrier, 3 + has_left.astype(jnp.int32) + has_right.astype(jnp.int32))

    def swap(c):
        return remote(
            clips_ref.at[0, 0, :, pixels(1 - y_lo, c)],
            window.at[2 + y_lo, c],
            swap_send.at[c],
            swap_recv.at[c],
            partner,
        )

    def swap_in(c):
        return remote(
            clips_ref.at[0, 0, :, pixels(y_lo, c)],
            window.at[3 - y_lo, c],
            swap_send.at[c],
            swap_recv.at[c],
            partner,
        )

    def deep_left(kind, c):
        which = y_lo if kind == 0 else 1 - y_lo
        return remote(
            clips_ref.at[0, 0, :, pixels(y_lo, c)] if kind == 0 else window.at[2 + which, c], window.at[4 + which, c], deep_send.at[0, kind, c], deep_recv.at[0, kind, c], left
        )

    def deep_right(kind, c):
        which = y_lo if kind == 0 else 1 - y_lo
        return remote(
            clips_ref.at[0, 0, :, pixels(y_lo, c)] if kind == 0 else window.at[2 + which, c], window.at[which, c], deep_send.at[1, kind, c], deep_recv.at[1, kind, c], right
        )

    def block(index, q):
        return wt.at[index, :, pl.ds(pl.multiple_of(q * LANES, LANES), LANES)]

    def own_to_sibling(index):
        return remote(wt.at[index], wt.at[index], own_send.at[0], own_recv.at[0], sibling)

    def to_across(index, q):
        return remote(block(index, q), block(index, q), cut_send.at[q], cut_recv.at[q], across)

    def to_partner(index, q):
        return remote(block(index, q), block(index, q), side_send.at[q], side_recv.at[q], partner)

    def to_sibling(index, q):
        return remote(block(index, q), block(index, q), sib_send.at[q], sib_recv.at[q], sibling)

    def forward_cut(i):
        q = 2 * i + y_lo
        to_across(gathered, q).wait_recv()
        to_partner(gathered, q).start()
        to_sibling(gathered, q).start()

    def forward_side(i):
        q = 2 * i + 1 - y_lo
        to_partner(gathered, q).wait_recv()
        to_sibling(gathered, q).start()

    def cross_all():
        for q in range(pieces):
            to_across(seg, q).start()

    def cross():
        for i in range(half):
            to_across(seg, 2 * i + 1 - y_lo).start()

    pl.when(source)(cross_all)

    for c in range(chunks):
        swap(c).start()
        at_left(lambda: deep_left(0, c).start())
        at_right(lambda: deep_right(0, c).start())

    pl.when(jnp.logical_not(source))(turn)
    own_to_sibling(seg).start()

    for load in loads[7:]:
        load.wait()
    row = lax.broadcasted_iota(jnp.int32, (EMB_ROWS, 1), 0)
    when = jnp.zeros((EMB_ROWS, 1), jnp.int32)
    for m in range(SECTIONS):
        when = jnp.where(row == m, time_smem[m], when)
    angle = when.astype(f32) * freq_vmem[...]
    lane = lax.broadcasted_iota(jnp.int32, angle.shape, 1)
    emb = jnp.where(lane < C // 2, jnp.sin(angle), jnp.cos(angle)).astype(bf16)
    loads[4].wait()
    film_rows[seg] = jnp.dot(emb, raw_film[...], preferred_element_type=f32)

    def film_copy(index, which, device):
        return remote(film_rows.at[index], film_rows.at[index], film_send.at[which], film_recv.at[which], device)

    film_copy(seg, 0, sibling).start()
    film_copy(seg, 1, across).start()

    def pass_film():
        film_copy(gathered, 1, across).wait_recv()
        film_copy(gathered, 2, sibling).start()

    def column(values):
        return jnp.broadcast_to(values, (LANES, C)).T

    def modulate(s):
        mine = jnp.sum(jnp.where(row == seg, film_rows[s], 0.0), axis=0, keepdims=True)
        film_col[s] = column(1.0 + mine)

    for s in range(SECTIONS):
        gain_col[s] = column(gain_vmem[s : s + 1, :])

    @pl.when(jnp.logical_not(has_left))
    def _():
        halo_l[...] = jnp.zeros_like(halo_l)
        window[0:2] = jnp.zeros((2, chunks, C, LANES), bf16)

    @pl.when(jnp.logical_not(has_right))
    def _():
        halo_r[...] = jnp.zeros_like(halo_r)
        window[4:6] = jnp.zeros((2, chunks, C, LANES), bf16)

    def normed(values, s):
        meansq = jnp.sum(values * values, axis=0, keepdims=True) * (1.0 / C)
        return (values * lax.rsqrt(meansq + 1e-05) * gain_col[s]).astype(bf16)

    def norm_frame(j, c):
        norm0[j, c] = normed(window[j, c].astype(f32), 0)

    def own_norms(c, carry):
        take(c).wait()
        norm_frame(2 + y_lo, c)
        return carry

    lax.fori_loop(0, chunks, own_norms, 0)
    pl.when(jnp.logical_or(y_hi == 1, core == 1))(cross)

    for load in loads[5:7]:
        load.wait()
    for n in range(2):
        for k in range(C // LANES + 1):
            lo, hi = k * LANES, min((k + 1) * LANES, C)
            skt[n, :, lo:hi] = raw_skip[n * C + lo : n * C + hi, :].T

    direct = {0: (0, 1, 2), 1: (3, 4, 5), 2: (6, 7, 8), 3: (9,)}
    cut_second = {1: (0, 1), 2: (2, 3), 3: (4,)}
    side_second = {3: (0, 1)}
    cut_later = {2: (0, 1), 3: (2, 3, 4)}
    side_later = {1: (0, 1), 2: (2, 3), 3: (4,)}

    def arrive(c, carry):
        swap_in(c).wait_recv()
        at_left(lambda: deep_left(1, c).start())
        at_right(lambda: deep_right(1, c).start())
        norm_frame(3 - y_lo, c)
        for at in range(chunks):

            @pl.when(jnp.logical_and(early, c == at))
            def _():
                for q in direct.get(at, ()):
                    to_across(gathered, q).wait_recv()
                    to_sibling(gathered, q).start()

        at_left(lambda: deep_right(0, c).wait_recv())
        norm_frame(y_lo, c)
        at_right(lambda: deep_left(0, c).wait_recv())
        norm_frame(4 + y_lo, c)
        for at in range(chunks):

            @pl.when(jnp.logical_and(second, c == at))
            def _():
                for i in cut_second.get(at, ()):
                    forward_cut(i)
                for i in side_second.get(at, ()):
                    forward_side(i)

            @pl.when(jnp.logical_and(y_hi == 0, c == at))
            def _():
                for i in cut_later.get(at, ()):
                    forward_cut(i)

        return carry

    lax.fori_loop(0, chunks, arrive, 0)
    pass_film()

    def await_section(s):
        @pl.when(sib_own == s)
        def _():
            own_to_sibling(sib_own).wait_recv()
            film_copy(sib_own, 0, sibling).wait_recv()

        @pl.when(relayed == s)
        def _():
            for q in range(pieces):
                to_sibling(relayed, q).wait_recv()
            film_copy(relayed, 2, sibling).wait_recv()

        modulate(s)

    pad = jnp.zeros((4 * C - 3 * C - 2 * LANES, 2 * LANES), bf16)

    def section(s, normals, base, skip=None):
        taps = [jnp.concatenate(normals[t : t + 2], axis=1) for t in range(3)]
        mixed = jnp.dot(wt[s, :, : 8 * LANES], jnp.concatenate(taps + [pad], axis=0), preferred_element_type=f32)
        scale = film_col[s]
        hidden = jax.nn.silu(mixed * jnp.concatenate([scale, scale], axis=1)).astype(bf16)
        weights = wt[s, :, 7 * LANES :]
        fields = [pad, hidden]
        if skip is not None:
            weights = jnp.concatenate([weights, skt[s - 2]], axis=1)
            fields = fields + [skip]
        total = base.astype(f32) + jnp.dot(weights, jnp.concatenate(fields, axis=0), preferred_element_type=f32)
        return total.astype(bf16)

    def to_left(s, c):
        return remote(
            nrm.at[s - 2, 0, c], halo_r.at[s - 2, c], halo_send.at[0, s - 2, c], halo_recv.at[1, s - 2, c], left
        )

    def to_right(s, c):
        return remote(
            nrm.at[s - 2, 1, c], halo_l.at[s - 2, c], halo_send.at[1, s - 2, c], halo_recv.at[0, s - 2, c], right
        )

    def keep(result, s, c):
        state[s - 1, 0, c] = result[:, :LANES]
        state[s - 1, 1, c] = result[:, LANES:]
        values = result.astype(f32)
        nrm[s - 2, 0, c] = normed(values[:, :LANES], s)
        at_left(lambda: to_left(s, c).start())
        nrm[s - 2, 1, c] = normed(values[:, LANES:], s)
        at_right(lambda: to_right(s, c).start())

    def frames_of(ref, j, c):
        return jnp.concatenate([ref[j, c], ref[j + 1, c]], axis=1)

    await_section(0)

    def deep_step(c, carry):
        at_left(lambda: deep_right(1, c).wait_recv())
        norm_frame(1 - y_lo, c)
        at_right(lambda: deep_left(1, c).wait_recv())
        norm_frame(5 - y_lo, c)
        low = section(0, [norm0[j, c] for j in range(0, 4)], frames_of(window, 1, c))
        state[0, 0, c] = low[:, LANES:]
        values = low.astype(f32)
        norm1[0] = jnp.where(has_left, normed(values[:, :LANES], 1), jnp.zeros((C, LANES), bf16))
        norm1[1] = normed(values[:, LANES:], 1)
        high = section(0, [norm0[j, c] for j in range(2, 6)], frames_of(window, 3, c))
        state[0, 1, c] = high[:, :LANES]
        values = high.astype(f32)
        norm1[2] = normed(values[:, :LANES], 1)
        norm1[3] = jnp.where(has_right, normed(values[:, LANES:], 1), jnp.zeros((C, LANES), bf16))

        @pl.when(c == 0)
        def _():
            @pl.when(second)
            def _():
                for i in range(2, half):
                    forward_side(i)

            await_section(1)

        keep(section(1, [norm1[j] for j in range(4)], frames_of(state.at[0], 0, c)), 2, c)
        for at in range(chunks):

            @pl.when(jnp.logical_and(y_hi == 0, c == at))
            def _():
                for i in side_later.get(at, ()):
                    forward_side(i)

        return carry

    lax.fori_loop(0, chunks, deep_step, 0)

    def back_out(c):
        return remote(
            give.at[c], out_ref.at[0, 0, :, pixels(y_lo, c)], back_send.at[c], back_recv.at[c], partner
        )

    def back_in(c):
        return remote(
            give.at[c], out_ref.at[0, 0, :, pixels(1 - y_lo, c)], back_send.at[c], back_recv.at[c], partner
        )

    for s in (2, 3):
        await_section(s)

        def step(c, carry):
            at_left(lambda: to_right(s, c).wait_recv())
            at_right(lambda: to_left(s, c).wait_recv())
            normals = [halo_l[s - 2, c], nrm[s - 2, 0, c], nrm[s - 2, 1, c], halo_r[s - 2, c]]
            skip = frames_of(state.at[0], 0, c) if s == 2 else frames_of(window, 2, c)
            result = section(s, normals, frames_of(state.at[s - 1], 0, c), skip)
            if s == 2:
                keep(result, 3, c)
            else:
                give[c] = jnp.where(y_lo == 0, result[:, LANES:], result[:, :LANES])
                back_out(c).start()
                out_ref[0, 0, :, pixels(y_lo, c)] = jnp.where(y_lo == 0, result[:, :LANES], result[:, LANES:])
            return carry

        lax.fori_loop(0, chunks, step, 0)

    def finish(c, carry):
        swap(c).wait_send()
        for kind in range(2):
            at_left(lambda: deep_left(kind, c).wait_send())
            at_right(lambda: deep_right(kind, c).wait_send())
        for s in (2, 3):
            at_left(lambda: to_left(s, c).wait_send())
            at_right(lambda: to_right(s, c).wait_send())
        return carry

    lax.fori_loop(0, chunks, finish, 0)
    own_to_sibling(seg).wait_send()
    for i in range(half):
        to_across(seg, 2 * i + 1 - y_lo).wait_send()

    @pl.when(jnp.logical_and(y_hi == 0, core == 0))
    def _():
        for i in range(half):
            to_across(seg, 2 * i + y_lo).wait_send()

    @pl.when(jnp.logical_not(early))
    def _():
        for i in range(half):
            to_partner(gathered, 2 * i + y_lo).wait_send()

    for q in range(pieces):
        to_sibling(gathered, q).wait_send()
    film_copy(seg, 0, sibling).wait_send()
    film_copy(seg, 1, across).wait_send()
    film_copy(gathered, 2, sibling).wait_send()

    def returned(c, carry):
        back_out(c).wait_send()
        back_in(c).wait_recv()
        return carry

    lax.fori_loop(0, chunks, returned, 0)


def shards(geometry, clips, timesteps, gain, temporal_weight, film_weight, out_weight, skip_weight):
    C, chunks, frames = geometry
    pieces = 4 * C // LANES
    base = np.exp(-math.log(10000.0) * np.arange(C // 2) / (C // 2))
    freq = jnp.asarray(np.concatenate([base, base])[None, :].astype(np.float32))
    hbm = pl.BlockSpec(memory_space=pltpu.HBM)
    bf16, f32 = jnp.bfloat16, jnp.float32
    dma = pltpu.SemaphoreType.DMA
    flops = 2 * 22 * C * C * 2 * chunks * LANES
    return pl.pallas_call(
        functools.partial(unet_kernel, geometry),
        out_shape=pltpu.VMEM(clips.shape, bf16),
        in_specs=[hbm] * 8,
        out_specs=pl.BlockSpec(memory_space=pltpu.VMEM),
        scratch_shapes=[
            pltpu.SMEM(timesteps.shape, jnp.int32),
            pltpu.VMEM(freq.shape, f32),
            pltpu.VMEM(gain.shape, f32),
            pltpu.VMEM((4 * C, C), bf16),
            pltpu.VMEM((2 * C, C), bf16),
            pltpu.VMEM((C, C), bf16),
            pltpu.VMEM((SECTIONS, C, 4 * C), bf16),
            pltpu.VMEM((2, C, C), bf16),
            pltpu.VMEM((SECTIONS, EMB_ROWS, C), f32),
            pltpu.VMEM((SECTIONS, C, LANES), f32),
            pltpu.VMEM((SECTIONS, C, LANES), f32),
            pltpu.VMEM((6, chunks, C, LANES), bf16),
            pltpu.VMEM((6, chunks, C, LANES), bf16),
            pltpu.VMEM((4, C, LANES), bf16),
            pltpu.VMEM((3, 2, chunks, C, LANES), bf16),
            pltpu.VMEM((2, 2, chunks, C, LANES), bf16),
            pltpu.VMEM((2, chunks, C, LANES), bf16),
            pltpu.VMEM((2, chunks, C, LANES), bf16),
            pltpu.VMEM((chunks, C, LANES), bf16),
            dma((10,)),
            dma((chunks,)),
            dma((chunks,)),
            dma((chunks,)),
            dma((2, 2, chunks)),
            dma((2, 2, chunks)),
            dma((2, 2, chunks)),
            dma((2, 2, chunks)),
            dma((1,)),
            dma((1,)),
            dma((pieces,)),
            dma((pieces,)),
            dma((pieces,)),
            dma((pieces,)),
            dma((pieces,)),
            dma((pieces,)),
            dma((3,)),
            dma((3,)),
            dma((chunks,)),
            dma((chunks,)),
        ],
        compiler_params=pltpu.CompilerParams(
            collective_id=0, has_side_effects=True, vmem_limit_bytes=60 * 10**6
        ),
        cost_estimate=pl.CostEstimate(flops=flops, bytes_accessed=4 * clips.size, transcendentals=0),
        name="unet",
    )(timesteps, freq, gain, temporal_weight, film_weight, out_weight, skip_weight, clips)


def solution(mesh):
    frames = mesh.shape["frame"]

    def run(clips, *rest):
        _, _, C, pix = clips.shape
        geometry = (C, pix // 2 // LANES, frames)
        return shards(geometry, clips, *rest)

    placed = (
        P("segment", "frame", None, None),
        P(),
        P(),
        P("segment", None, None, None),
        P("segment", None, None),
        P("segment", None, None),
        P(),
    )
    return jax.shard_map(
        run,
        mesh=mesh,
        in_specs=placed,
        out_specs=P("segment", "frame", None, None),
        check_vma=False,
    )
```

time: 56 us -> 52.5 us (0.938)
  Pallas kernels: 53.6 us -> 51.3 us
  local copies, waits for them, and re-layouts: 1.97 us -> 0.84 us
    pallas_call x1, Pallas kernels: 53.6 us -> 51.3 us  [shards(): pl.pallas_call(functools.partial(unet_kernel, geometry), out_shape=pltpu....]
    unnamed x1, local copies, waits for them, and re-layouts: 1.97 us -> 0.84 us
where the time goes in v3:
time: 52.5 us; the launch traced here: 52.1 us
  Pallas kernels  51.3 us (98%)
  local copies, waits for them, and re-layouts  0.84 us (2%)
    pallas_call x1, Pallas kernels, shards(): pl.pallas_call(functools.partial(unet_kernel, geometry), out_shape=pltpu....  51.3 us

profile of v3, /device:TPU:18, one launch (start us, length us, event | category | flops | bytes accessed | tf_op | source)
XLA Modules:
  0.0 52.1 jit_solution(3980123613857488108)
XLA Ops:
  0.0 51.3 %unet.1 = bf16[1,1,320,1024]{3,2,1,0:T(8,128)(2,1)S(1)} custom-call(s32[4]{0:T(128)} %time_ref.1, f32[1,320]{1,0:T(1,128)} %constant.2.clone.freq_ref, f32[4,320]{1,0:T(4,128)} %gain_ref.1, bf16[1,3,320,320]{3,2,1,0:T(8,128)(2,1)} %taps_ref.1, bf16[1,320,320]{2,1,0:T(8,128)(2,1)} %film_ref.1, bf16[1,320,320]{2,1,0:T(8,128)(2,1)} %proj_ref.1, ...), custom_call_target="tpu_custom_call" | custom-call | flops 4613734400 | bytes 1310720 | tf_op jit(solution)/shard_map/unet/pallas_call | solution.py:498
  51.3 0.8 %copy.10 = bf16[1,1,320,1024]{3,2,1,0:T(8,128)(2,1)} copy(bf16[1,1,320,1024]{3,2,1,0:T(8,128)(2,1)S(1)} %unet.1) | data formatting | bytes 1310720

commit v4 on v3

--- a/solution.py
+++ b/solution.py
@@ -13,6 +13,7 @@
 LANES = 128
 SECTIONS = 4
 EMB_ROWS = 8
+SHARED = 4
 
 
 def unet_kernel(
@@ -68,7 +69,7 @@
 ):
     C, chunks, frames = geometry
     pieces = 4 * C // LANES
-    half = pieces // 2
+    direct = pieces - SHARED
     half_pix = chunks * LANES
     groups = frames // 2
     f32, bf16 = jnp.float32, jnp.bfloat16
@@ -83,6 +84,12 @@
     right = (seg, frame + 2)
     sibling = (y_hi * 2 + 1 - core, frame)
     across = ((1 - y_hi) * 2 + core, group * 2 + 1 - y_lo)
+    x_step = 16 if frames >= 32 else 2
+    spread = frames // x_step
+    x_par = (frame // x_step) % 2
+    turn_x = jnp.where((frame % x_step) // 2 == x_step // 2 - 1, 1, spread - 1)
+    ahead = (seg, (frame + x_step * turn_x) % frames)
+    behind = (seg, (frame + x_step * (spread - turn_x)) % frames)
     has_left = group > 0
     has_right = group < groups - 1
     gathered = (1 - y_hi) * 2 + core
@@ -137,6 +144,11 @@
     for device in (partner, sibling, across):
         pl.semaphore_signal(barrier, inc=1, device_id=device, device_id_type=MESH)
 
+    @pl.when(early)
+    def _():
+        for device in (ahead, behind):
+            pl.semaphore_signal(barrier, inc=1, device_id=device, device_id_type=MESH)
+
     def turn():
         for load in loads[:4]:
             load.wait()
@@ -146,7 +158,7 @@
     source = jnp.logical_and(y_hi == 0, core == 0)
     pl.when(source)(turn)
 
-    pl.semaphore_wait(barrier, 3 + has_left.astype(jnp.int32) + has_right.astype(jnp.int32))
+    pl.semaphore_wait(barrier, 3 + 2 * early.astype(jnp.int32) + has_left.astype(jnp.int32) + has_right.astype(jnp.int32))
 
     def swap(c):
         return remote(
@@ -193,26 +205,46 @@
     def to_sibling(index, q):
         return remote(block(index, q), block(index, q), sib_send.at[q], sib_recv.at[q], sibling)
 
+    def to_ahead(index, q):
+        return remote(block(index, q), block(index, q), side_send.at[q], side_recv.at[q], ahead)
+
+    def order(parity, i):
+        return i + parity * (pieces - 1 - 2 * i)
+
+    def first_cut(i):
+        q = order(x_par, i)
+        to_across(gathered, q).wait_recv()
+        if i < SHARED:
+            to_ahead(gathered, q).start()
+        to_sibling(gathered, q).start()
+
+    def first_side(i):
+        q = order(1 - x_par, i)
+        to_ahead(gathered, q).wait_recv()
+        to_sibling(gathered, q).start()
+
     def forward_cut(i):
-        q = 2 * i + y_lo
+        q = order(y_lo, i)
         to_across(gathered, q).wait_recv()
-        to_partner(gathered, q).start()
+        if i < SHARED:
+            to_partner(gathered, q).start()
         to_sibling(gathered, q).start()
 
     def forward_side(i):
-        q = 2 * i + 1 - y_lo
+        q = order(1 - y_lo, i)
         to_partner(gathered, q).wait_recv()
         to_sibling(gathered, q).start()
 
-    def cross_all():
-        for q in range(pieces):
-            to_across(seg, q).start()
+    def cross_first():
+        for i in range(direct):
+            to_across(seg, order(x_par, i)).start()
 
     def cross():
-        for i in range(half):
-            to_across(seg, 2 * i + 1 - y_lo).start()
-
-    pl.when(source)(cross_all)
+        for i in range(direct):
+            to_across(seg, order(1 - y_lo, i)).start()
+
+    shares = range(SHARED)
+    pl.when(source)(cross_first)
 
     for c in range(chunks):
         swap(c).start()
@@ -277,7 +309,7 @@
         return carry
 
     lax.fori_loop(0, chunks, own_norms, 0)
-    pl.when(jnp.logical_or(y_hi == 1, core == 1))(cross)
+    pl.when(early)(cross)
 
     for load in loads[5:7]:
         load.wait()
@@ -286,11 +318,8 @@
             lo, hi = k * LANES, min((k + 1) * LANES, C)
             skt[n, :, lo:hi] = raw_skip[n * C + lo : n * C + hi, :].T
 
-    direct = {0: (0, 1, 2), 1: (3, 4, 5), 2: (6, 7, 8), 3: (9,)}
-    cut_second = {1: (0, 1), 2: (2, 3), 3: (4,)}
-    side_second = {3: (0, 1)}
-    cut_later = {2: (0, 1), 3: (2, 3, 4)}
-    side_later = {1: (0, 1), 2: (2, 3), 3: (4,)}
+    first_plan = {0: (0, 1, 2), 1: (3, 4), 2: range(5, direct)}
+    later_plan = {2: (0, 1, 2), 3: (3, 4, 5)}
 
     def arrive(c, carry):
         swap_in(c).wait_recv()
@@ -301,27 +330,29 @@
 
             @pl.when(jnp.logical_and(early, c == at))
             def _():
-                for q in direct.get(at, ()):
-                    to_across(gathered, q).wait_recv()
-                    to_sibling(gathered, q).start()
-
+                for i in first_plan.get(at, ()):
+                    first_cut(i)
+                if at == 2:
+                    for i in shares:
+                        first_side(i)
+
+        pl.when(jnp.logical_and(patient, c == 0))(cross)
         at_left(lambda: deep_right(0, c).wait_recv())
         norm_frame(y_lo, c)
         at_right(lambda: deep_left(0, c).wait_recv())
         norm_frame(4 + y_lo, c)
         for at in range(chunks):
 
-            @pl.when(jnp.logical_and(second, c == at))
+            @pl.when(jnp.logical_and(source, c == at))
             def _():
-                for i in cut_second.get(at, ()):
+                for i in later_plan.get(at, ()):
                     forward_cut(i)
-                for i in side_second.get(at, ()):
-                    forward_side(i)
-
-            @pl.when(jnp.logical_and(y_hi == 0, c == at))
-            def _():
-                for i in cut_later.get(at, ()):
-                    forward_cut(i)
+
+        @pl.when(jnp.logical_and(second, c == chunks - 1))
+        def _():
+            cross()
+            for i in shares:
+                forward_cut(i)
 
         return carry
 
@@ -342,15 +373,19 @@
 
         modulate(s)
 
-    pad = jnp.zeros((4 * C - 3 * C - 2 * LANES, 2 * LANES), bf16)
-
-    def section(s, normals, base, skip=None):
-        taps = [jnp.concatenate(normals[t : t + 2], axis=1) for t in range(3)]
-        mixed = jnp.dot(wt[s, :, : 8 * LANES], jnp.concatenate(taps + [pad], axis=0), preferred_element_type=f32)
-        scale = film_col[s]
-        hidden = jax.nn.silu(mixed * jnp.concatenate([scale, scale], axis=1)).astype(bf16)
+    def section(s, normals, base, skip=None, parts=1):
+        count = len(normals) - 2
+        pad = jnp.zeros((4 * C - 3 * C - 2 * LANES, count * LANES), bf16)
+        taps = [jnp.concatenate(normals[t : t + count], axis=1) for t in range(3)]
+        stacked = jnp.concatenate(taps + [pad], axis=0)
+        hidden = []
+        for part in range(parts):
+            rows = slice(part * C // parts, (part + 1) * C // parts)
+            mixed = jnp.dot(wt[s, rows, : 8 * LANES], stacked, preferred_element_type=f32)
+            scale = jnp.concatenate([film_col[s, rows]] * count, axis=1)
+            hidden.append(jax.nn.silu(mixed * scale).astype(bf16))
         weights = wt[s, :, 7 * LANES :]
-        fields = [pad, hidden]
+        fields = [pad] + hidden
         if skip is not None:
             weights = jnp.concatenate([weights, skt[s - 2]], axis=1)
             fields = fields + [skip]
@@ -386,33 +421,38 @@
         norm_frame(1 - y_lo, c)
         at_right(lambda: deep_left(1, c).wait_recv())
         norm_frame(5 - y_lo, c)
-        low = section(0, [norm0[j, c] for j in range(0, 4)], frames_of(window, 1, c))
-        state[0, 0, c] = low[:, LANES:]
-        values = low.astype(f32)
-        norm1[0] = jnp.where(has_left, normed(values[:, :LANES], 1), jnp.zeros((C, LANES), bf16))
-        norm1[1] = normed(values[:, LANES:], 1)
-        high = section(0, [norm0[j, c] for j in range(2, 6)], frames_of(window, 3, c))
-        state[0, 1, c] = high[:, :LANES]
-        values = high.astype(f32)
-        norm1[2] = normed(values[:, :LANES], 1)
-        norm1[3] = jnp.where(has_right, normed(values[:, LANES:], 1), jnp.zeros((C, LANES), bf16))
+        base = jnp.concatenate([window[j, c] for j in range(1, 5)], axis=1)
+        wide = section(0, [norm0[j, c] for j in range(6)], base)
+        state[0, 0, c] = wide[:, LANES : 2 * LANES]
+        state[0, 1, c] = wide[:, 2 * LANES : 3 * LANES]
+        values = wide.astype(f32)
+        nothing = jnp.zeros((C, LANES), bf16)
+        norm1[0] = jnp.where(has_left, normed(values[:, :LANES], 1), nothing)
+        norm1[1] = normed(values[:, LANES : 2 * LANES], 1)
+        norm1[2] = normed(values[:, 2 * LANES : 3 * LANES], 1)
+        norm1[3] = jnp.where(has_right, normed(values[:, 3 * LANES :], 1), nothing)
 
         @pl.when(c == 0)
         def _():
             @pl.when(second)
             def _():
-                for i in range(2, half):
+                for i in range(SHARED, direct):
+                    forward_cut(i)
+                for i in shares:
                     forward_side(i)
 
             await_section(1)
 
-        keep(section(1, [norm1[j] for j in range(4)], frames_of(state.at[0], 0, c)), 2, c)
-        for at in range(chunks):
-
-            @pl.when(jnp.logical_and(y_hi == 0, c == at))
-            def _():
-                for i in side_later.get(at, ()):
-                    forward_side(i)
+        keep(section(1, [norm1[j] for j in range(4)], frames_of(state.at[0], 0, c), parts=2), 2, c)
+        @pl.when(jnp.logical_and(source, c == 0))
+        def _():
+            for i in range(6, direct):
+                forward_cut(i)
+
+        @pl.when(jnp.logical_and(source, c == 1))
+        def _():
+            for i in shares:
+                forward_side(i)
 
         return carry
 
@@ -436,9 +476,25 @@
             at_right(lambda: to_left(s, c).wait_recv())
             normals = [halo_l[s - 2, c], nrm[s - 2, 0, c], nrm[s - 2, 1, c], halo_r[s - 2, c]]
             skip = frames_of(state.at[0], 0, c) if s == 2 else frames_of(window, 2, c)
-            result = section(s, normals, frames_of(state.at[s - 1], 0, c), skip)
+            result = section(s, normals, frames_of(state.at[s - 1], 0, c), skip, parts=2)
             if s == 2:
                 keep(result, 3, c)
+
+                @pl.when(jnp.logical_and(patient, c == 0))
+                def _():
+                    for i in shares:
+                        forward_cut(i)
+
+                @pl.when(jnp.logical_and(patient, c == 1))
+                def _():
+                    for i in range(SHARED, direct):
+                        forward_cut(i)
+
+                @pl.when(jnp.logical_and(patient, c == 2))
+                def _():
+                    for i in shares:
+                        forward_side(i)
+
             else:
                 give[c] = jnp.where(y_lo == 0, result[:, LANES:], result[:, :LANES])
                 back_out(c).start()
@@ -459,18 +515,25 @@
 
     lax.fori_loop(0, chunks, finish, 0)
     own_to_sibling(seg).wait_send()
-    for i in range(half):
-        to_across(seg, 2 * i + 1 - y_lo).wait_send()
-
-    @pl.when(jnp.logical_and(y_hi == 0, core == 0))
+    @pl.when(source)
     def _():
-        for i in range(half):
-            to_across(seg, 2 * i + y_lo).wait_send()
+        for i in range(direct):
+            to_across(seg, order(x_par, i)).wait_send()
+
+    @pl.when(jnp.logical_not(source))
+    def _():
+        for i in range(direct):
+            to_across(seg, order(1 - y_lo, i)).wait_send()
+
+    @pl.when(early)
+    def _():
+        for i in shares:
+            to_ahead(gathered, order(x_par, i)).wait_send()
 
     @pl.when(jnp.logical_not(early))
     def _():
-        for i in range(half):
-            to_partner(gathered, 2 * i + y_lo).wait_send()
+        for i in shares:
+            to_partner(gathered, order(y_lo, i)).wait_send()
 
     for q in range(pieces):
         to_sibling(gathered, q).wait_send()

time: 52.5 us -> 48.9 us (0.931)
  Pallas kernels: 51.3 us -> 48 us
    pallas_call x1, Pallas kernels: 51.3 us -> 48 us  [shards(): pl.pallas_call(functools.partial(unet_kernel, geometry), out_shape=pltpu....]
where the time goes in v4:
time: 48.9 us; the launch traced here: 48.8 us
  Pallas kernels  48 us (98%)
  local copies, waits for them, and re-layouts  0.84 us (2%)
    pallas_call x1, Pallas kernels, shards(): pl.pallas_call(functools.partial(unet_kernel, geometry), out_shape=pltpu....  48 us

profile of v4, /device:TPU:18, one launch (start us, length us, event | category | flops | bytes accessed | tf_op | source)
XLA Modules:
  0.0 48.8 jit_solution(10861230520683888466)
XLA Ops:
  0.0 48.0 %unet.1 = bf16[1,1,320,1024]{3,2,1,0:T(8,128)(2,1)S(1)} custom-call(s32[4]{0:T(128)} %time_ref.1, f32[1,320]{1,0:T(1,128)} %constant.2.clone.freq_ref, f32[4,320]{1,0:T(4,128)} %gain_ref.1, bf16[1,3,320,320]{3,2,1,0:T(8,128)(2,1)} %taps_ref.1, bf16[1,320,320]{2,1,0:T(8,128)(2,1)} %film_ref.1, bf16[1,320,320]{2,1,0:T(8,128)(2,1)} %proj_ref.1, ...), custom_call_target="tpu_custom_call" | custom-call | flops 4613734400 | bytes 1310720 | tf_op jit(solution)/shard_map/unet/pallas_call | solution.py:561
  48.0 0.8 %copy.10 = bf16[1,1,320,1024]{3,2,1,0:T(8,128)(2,1)} copy(bf16[1,1,320,1024]{3,2,1,0:T(8,128)(2,1)S(1)} %unet.1) | data formatting | bytes 1310720

commit v5 on v4

--- a/solution.py
+++ b/solution.py
@@ -252,7 +252,7 @@
         at_right(lambda: deep_right(0, c).start())
 
     pl.when(jnp.logical_not(source))(turn)
-    own_to_sibling(seg).start()
+    pl.when(y_hi == 0)(lambda: own_to_sibling(seg).start())
 
     for load in loads[7:]:
         load.wait()
@@ -311,13 +311,6 @@
     lax.fori_loop(0, chunks, own_norms, 0)
     pl.when(early)(cross)
 
-    for load in loads[5:7]:
-        load.wait()
-    for n in range(2):
-        for k in range(C // LANES + 1):
-            lo, hi = k * LANES, min((k + 1) * LANES, C)
-            skt[n, :, lo:hi] = raw_skip[n * C + lo : n * C + hi, :].T
-
     first_plan = {0: (0, 1, 2), 1: (3, 4), 2: range(5, direct)}
     later_plan = {2: (0, 1, 2), 3: (3, 4, 5)}
 
@@ -336,7 +329,7 @@
                     for i in shares:
                         first_side(i)
 
-        pl.when(jnp.logical_and(patient, c == 0))(cross)
+        pl.when(jnp.logical_and(patient, c == 2))(cross)
         at_left(lambda: deep_right(0, c).wait_recv())
         norm_frame(y_lo, c)
         at_right(lambda: deep_left(0, c).wait_recv())
@@ -358,6 +351,14 @@
 
     lax.fori_loop(0, chunks, arrive, 0)
     pass_film()
+    pl.when(y_hi == 1)(lambda: own_to_sibling(seg).start())
+    for load in loads[5:7]:
+        load.wait()
+    for n in range(2):
+        for k in range(C // LANES + 1):
+            lo, hi = k * LANES, min((k + 1) * LANES, C)
+            skt[n, :, lo:hi] = raw_skip[n * C + lo : n * C + hi, :].T
+
 
     def await_section(s):
         @pl.when(sib_own == s)

time: 48.9 us -> 46.3 us (0.947)
  Pallas kernels: 48 us -> 45.3 us
    pallas_call x1, Pallas kernels: 48 us -> 45.3 us  [shards(): pl.pallas_call(functools.partial(unet_kernel, geometry), out_shape=pltpu....]
where the time goes in v5:
time: 46.3 us; the launch traced here: 46.2 us
  Pallas kernels  45.3 us (98%)
  local copies, waits for them, and re-layouts  0.84 us (2%)
    pallas_call x1, Pallas kernels, shards(): pl.pallas_call(functools.partial(unet_kernel, geometry), out_shape=pltpu....  45.3 us

profile of v5, /device:TPU:18, one launch (start us, length us, event | category | flops | bytes accessed | tf_op | source)
XLA Modules:
  0.0 46.2 jit_solution(14990198402525133837)
XLA Ops:
  0.0 45.3 %unet.1 = bf16[1,1,320,1024]{3,2,1,0:T(8,128)(2,1)S(1)} custom-call(s32[4]{0:T(128)} %time_ref.1, f32[1,320]{1,0:T(1,128)} %constant.2.clone.freq_ref, f32[4,320]{1,0:T(4,128)} %gain_ref.1, bf16[1,3,320,320]{3,2,1,0:T(8,128)(2,1)} %taps_ref.1, bf16[1,320,320]{2,1,0:T(8,128)(2,1)} %film_ref.1, bf16[1,320,320]{2,1,0:T(8,128)(2,1)} %proj_ref.1, ...), custom_call_target="tpu_custom_call" | custom-call | flops 4613734400 | bytes 1310720 | tf_op jit(solution)/shard_map/unet/pallas_call | solution.py:562
  45.4 0.8 %copy.10 = bf16[1,1,320,1024]{3,2,1,0:T(8,128)(2,1)} copy(bf16[1,1,320,1024]{3,2,1,0:T(8,128)(2,1)S(1)} %unet.1) | data formatting | bytes 1310720

commit v6 on v5

--- a/solution.py
+++ b/solution.py
@@ -251,7 +251,7 @@
         at_left(lambda: deep_left(0, c).start())
         at_right(lambda: deep_right(0, c).start())
 
-    pl.when(jnp.logical_not(source))(turn)
+    pl.when(patient)(turn)
     pl.when(y_hi == 0)(lambda: own_to_sibling(seg).start())
 
     for load in loads[7:]:
@@ -309,6 +309,7 @@
         return carry
 
     lax.fori_loop(0, chunks, own_norms, 0)
+    pl.when(y_hi == 1)(turn)
     pl.when(early)(cross)
 
     first_plan = {0: (0, 1, 2), 1: (3, 4), 2: range(5, direct)}

time: 46.3 us -> 46.3 us (level)
  no operation moved by 1% of the time
where the time goes in v6:
time: 46.3 us; the launch traced here: 46.2 us
  Pallas kernels  45.3 us (98%)
  local copies, waits for them, and re-layouts  0.84 us (2%)
    pallas_call x1, Pallas kernels, shards(): pl.pallas_call(functools.partial(unet_kernel, geometry), out_shape=pltpu....  45.3 us

profile of v6, /device:TPU:18, one launch (start us, length us, event | category | flops | bytes accessed | tf_op | source)
XLA Modules:
  0.0 46.2 jit_solution(16165583196383437833)
XLA Ops:
  0.0 45.3 %unet.1 = bf16[1,1,320,1024]{3,2,1,0:T(8,128)(2,1)S(1)} custom-call(s32[4]{0:T(128)} %time_ref.1, f32[1,320]{1,0:T(1,128)} %constant.2.clone.freq_ref, f32[4,320]{1,0:T(4,128)} %gain_ref.1, bf16[1,3,320,320]{3,2,1,0:T(8,128)(2,1)} %taps_ref.1, bf16[1,320,320]{2,1,0:T(8,128)(2,1)} %film_ref.1, bf16[1,320,320]{2,1,0:T(8,128)(2,1)} %proj_ref.1, ...), custom_call_target="tpu_custom_call" | custom-call | flops 4613734400 | bytes 1310720 | tf_op jit(solution)/shard_map/unet/pallas_call | solution.py:563
  45.4 0.8 %copy.10 = bf16[1,1,320,1024]{3,2,1,0:T(8,128)(2,1)} copy(bf16[1,1,320,1024]{3,2,1,0:T(8,128)(2,1)S(1)} %unet.1) | data formatting | bytes 1310720

commit v7 on v5

--- a/solution.py
+++ b/solution.py
@@ -251,8 +251,7 @@
         at_left(lambda: deep_left(0, c).start())
         at_right(lambda: deep_right(0, c).start())
 
-    pl.when(jnp.logical_not(source))(turn)
-    pl.when(y_hi == 0)(lambda: own_to_sibling(seg).start())
+    pl.when(source)(lambda: own_to_sibling(seg).start())
 
     for load in loads[7:]:
         load.wait()
@@ -309,6 +308,8 @@
         return carry
 
     lax.fori_loop(0, chunks, own_norms, 0)
+    pl.when(jnp.logical_not(source))(turn)
+    pl.when(patient)(lambda: own_to_sibling(seg).start())
     pl.when(early)(cross)
 
     first_plan = {0: (0, 1, 2), 1: (3, 4), 2: range(5, direct)}

time: 46.3 us -> 46.3 us (level)
  no operation moved by 1% of the time
where the time goes in v7:
time: 46.3 us; the launch traced here: 46.2 us
  Pallas kernels  45.3 us (98%)
  local copies, waits for them, and re-layouts  0.84 us (2%)
    pallas_call x1, Pallas kernels, shards(): pl.pallas_call(functools.partial(unet_kernel, geometry), out_shape=pltpu....  45.3 us

profile of v7, /device:TPU:18, one launch (start us, length us, event | category | flops | bytes accessed | tf_op | source)
XLA Modules:
  0.0 46.2 jit_solution(1742772827077589559)
XLA Ops:
  0.0 45.3 %unet.1 = bf16[1,1,320,1024]{3,2,1,0:T(8,128)(2,1)S(1)} custom-call(s32[4]{0:T(128)} %time_ref.1, f32[1,320]{1,0:T(1,128)} %constant.2.clone.freq_ref, f32[4,320]{1,0:T(4,128)} %gain_ref.1, bf16[1,3,320,320]{3,2,1,0:T(8,128)(2,1)} %taps_ref.1, bf16[1,320,320]{2,1,0:T(8,128)(2,1)} %film_ref.1, bf16[1,320,320]{2,1,0:T(8,128)(2,1)} %proj_ref.1, ...), custom_call_target="tpu_custom_call" | custom-call | flops 4613734400 | bytes 1310720 | tf_op jit(solution)/shard_map/unet/pallas_call | solution.py:563
  45.4 0.8 %copy.10 = bf16[1,1,320,1024]{3,2,1,0:T(8,128)(2,1)} copy(bf16[1,1,320,1024]{3,2,1,0:T(8,128)(2,1)S(1)} %unet.1) | data formatting | bytes 1310720
